TPU v7x, 32 devices: a whole 2x2x4 slice. The times are simulated.
32 devices in a mesh: parts: 2 (over x), ep: 16 (over z, y, core).
Axes of the slice: x: 2, y: 2, z: 4, core: 2. Of those that a mesh axis runs over, the one named last changes fastest.
Arguments:
- queries: bfloat16 [1024, 8192], P(('parts', 'ep')), parts along dimension 0, may hold values from -128 to 128
- fresh_token_keys: bfloat16 [1024, 512], P(('parts', 'ep')), parts along dimension 0, may hold values from -4 to 4
- fresh_token_values: bfloat16 [1024, 512], P(('parts', 'ep')), parts along dimension 0, may hold values from -6 to 6
- pooled_keys: bfloat16 [8192, 16, 512], P(('parts', 'ep')), parts along dimension 0, may hold values from -6 to 6
- pooled_values: bfloat16 [8192, 16, 512], P(('parts', 'ep')), parts along dimension 0, may hold values from -6 to 6
- lengths: int32 [32, 32], P(('parts', 'ep')), parts along dimension 0, may hold values from 1 to 256, 3584 in all within a row
- page_order: int32 [32, 256], P(('parts', 'ep')), parts along dimension 0, may hold values from 0 to 255, each once within a row
- hidden: bfloat16 [1024, 4096], P(('parts', 'ep')), parts along dimension 0, may hold values from -40 to 40
- out_weight: bfloat16 [8192, 4096], P('ep'), may hold values from -1.25 to 1.25
- norm_gain: float32 [4096], replicated, may hold values from 0.25 to 1.75
- expert_ids: int32 [1024, 8], P(('parts', 'ep')), parts along dimension 0, may hold values from 0 to 15, all different within a row; in each aligned block of 32 rows (0 to 31, 32 to 63, ...) at most 16 rows name the same one
- gate_weights: float32 [1024, 8], P(('parts', 'ep')), parts along dimension 0, may hold values from 0.05 to 0.5
- expert_gate_up: bfloat16 [16, 4096, 1536], P('ep'), may hold values from -0.09375 to 0.09375
- expert_down: bfloat16 [16, 768, 4096], P('ep'), may hold values from -0.21875 to 0.21875
- mig_pages: int32 [32, 16], P(('parts', 'ep')), parts along dimension 0, may hold values from 0 to 255
- mig_dest: int32 [512, 1], P(('parts', 'ep')), parts along dimension 0, may hold values from 0 to 15; in each aligned block of 16 rows (0 to 15, 16 to 31, ...) no two rows name the same one
Outputs:
- layer_out: bfloat16 [1024, 4096], P(('parts', 'ep')), parts along dimension 0
- arrived_keys: bfloat16 [512, 16, 512], P(('parts', 'ep')), parts along dimension 0
- arrived_values: bfloat16 [512, 16, 512], P(('parts', 'ep')), parts along dimension 0
There are 2 independent parts, one for each index of `parts`. A program takes and returns all parts, laid end to end along the dimension named above; an argument that names none is the same for every part. Nothing has to cross between parts.
Inputs may be any that keep to these rules, and one draw needn't show every extreme that they name: `lengths`: the 32 sequences of one device hold (224) * 16 cached tokens together. `page_order`: each row is a permutation of the device's pool pages. `expert_ids`: each row names 8 different experts; among the rows of one device no expert is named more than 16 times. `mig_dest`: among the rows of one device no destination is named twice.
All inputs are finite; a program needn't handle non-finite values.
Results may differ from a plain program's by a relative error of at most 0.0075.
Values may be sent and summed in bfloat16 or wider, within the bound.
A program may use at most 128 MiB of HBM per device.

v0:
```python
import math

import jax
import jax.numpy as jnp
from jax import lax
from jax.sharding import PartitionSpec as P

QUERY_HEADS = 64
KEY_VALUE_HEADS = 4
HEAD_SIZE = 128
FFW = 768
TOPK = 8
PAGE_TOKENS = 16
MOST_SEQ_PAGES = 16
CAP = 16


def attend_local(
    queries, fresh_token_keys, fresh_token_values, pooled_keys, pooled_values, lengths, page_order
):
    sequence_count = queries.shape[0]
    pages_dev = page_order.shape[0]
    counts = (lengths + (PAGE_TOKENS - 1)) // PAGE_TOKENS
    starts = jnp.cumsum(counts) - counts
    logical = starts[:, None] + jnp.arange(MOST_SEQ_PAGES, dtype=jnp.int32)[None, :]
    physical_page = page_order[jnp.clip(logical, 0, pages_dev - 1)]
    every_key = pooled_keys[physical_page].reshape(
        sequence_count, MOST_SEQ_PAGES * PAGE_TOKENS, KEY_VALUE_HEADS, HEAD_SIZE
    )
    every_value = pooled_values[physical_page].reshape(
        sequence_count, MOST_SEQ_PAGES * PAGE_TOKENS, KEY_VALUE_HEADS, HEAD_SIZE
    )
    live = jnp.arange(MOST_SEQ_PAGES * PAGE_TOKENS, dtype=jnp.int32)[None, :] < lengths[:, None]
    grouped_queries = queries.reshape(
        sequence_count, KEY_VALUE_HEADS, QUERY_HEADS // KEY_VALUE_HEADS, HEAD_SIZE
    )
    scale_factor = 1.0 / math.sqrt(HEAD_SIZE)
    scores = (
        jnp.einsum(
            "shgd,sthd->shgt", grouped_queries, every_key, preferred_element_type=jnp.float32
        )
        * scale_factor
    )
    scores = jnp.where(live[:, None, None, :], scores, -1e30)
    self_score = (
        jnp.einsum(
            "fyvj,fyj->fyv",
            grouped_queries,
            fresh_token_keys.reshape(sequence_count, KEY_VALUE_HEADS, HEAD_SIZE),
            preferred_element_type=jnp.float32,
        )
        * scale_factor
    )
    highest = jnp.maximum(jnp.max(scores, -1), self_score)
    weights = jnp.exp(scores - highest[..., None])
    own_weight = jnp.exp(self_score - highest)
    total = jnp.sum(weights, -1) + own_weight
    probs = (weights / total[..., None]).astype(jnp.bfloat16)
    self_probability = (own_weight / total).astype(jnp.bfloat16)
    mixed_output = jnp.einsum(
        "shgt,sthd->shgd", probs, every_value, preferred_element_type=jnp.float32
    )
    mixed_output = mixed_output + self_probability.astype(jnp.float32)[
        ..., None
    ] * fresh_token_values.reshape(sequence_count, KEY_VALUE_HEADS, 1, HEAD_SIZE).astype(
        jnp.float32
    )
    return mixed_output.reshape(sequence_count, QUERY_HEADS * HEAD_SIZE).astype(jnp.bfloat16)


def on_device(
    queries,
    fresh_token_keys,
    fresh_token_values,
    pooled_keys,
    pooled_values,
    lengths,
    page_order,
    hidden,
    out_weight,
    norm_gain,
    expert_ids,
    gate_weights,
    expert_gate_up,
    expert_down,
    mig_pages,
    mig_dest,
):
    devices = lax.axis_size("ep")
    sequence_count = queries.shape[0]
    moved_keys = pooled_keys[mig_pages[0]]
    moved_values = pooled_values[mig_pages[0]]
    targets = (mig_dest[:, 0][:, None] == jnp.arange(devices, dtype=jnp.int32)[None, :]).astype(
        jnp.bfloat16
    )
    send_keys = jnp.einsum(
        "mt,mpw->tpw", targets, moved_keys, preferred_element_type=jnp.float32
    ).astype(jnp.bfloat16)
    send_values = jnp.einsum(
        "mt,mpw->tpw", targets, moved_values, preferred_element_type=jnp.float32
    ).astype(jnp.bfloat16)
    arrived_keys, arrived_values = (
        lax.all_to_all(send_keys, "ep", split_axis=0, concat_axis=0, tiled=True),
        lax.all_to_all(send_values, "ep", split_axis=0, concat_axis=0, tiled=True),
    )
    attended = attend_local(
        queries,
        fresh_token_keys,
        fresh_token_values,
        pooled_keys,
        pooled_values,
        lengths[0],
        page_order[0],
    )
    head_rows = lax.all_to_all(attended, "ep", split_axis=1, concat_axis=0, tiled=True)
    projected = lax.psum_scatter(
        jnp.dot(head_rows, out_weight, preferred_element_type=jnp.float32),
        "ep",
        scatter_dimension=0,
        tiled=True,
    )
    mid = (hidden.astype(jnp.float32) + projected).astype(jnp.bfloat16)
    mid_f = mid.astype(jnp.float32)
    normed = (
        mid_f * lax.rsqrt(jnp.mean(mid_f * mid_f, -1, keepdims=True) + 1e-06) * norm_gain
    ).astype(jnp.bfloat16)
    flat_ids = expert_ids.reshape(-1)
    assignments = flat_ids.shape[0]
    hits = (flat_ids[:, None] == jnp.arange(devices, dtype=jnp.int32)[None, :]).astype(jnp.int32)
    earlier = jnp.cumsum(hits, 0) - hits
    position = jnp.sum(earlier * hits, 1)
    slot = flat_ids * CAP + position
    slot_hot = (slot[:, None] == jnp.arange(devices * CAP, dtype=jnp.int32)[None, :]).astype(
        jnp.float32
    )
    owner_tok = jnp.arange(assignments, dtype=jnp.int32) // TOPK
    token_hot = (owner_tok[:, None] == jnp.arange(sequence_count, dtype=jnp.int32)[None, :]).astype(
        jnp.float32
    )
    mixing = jnp.dot(
        (token_hot * gate_weights.reshape(-1)[:, None]).T, slot_hot, precision=lax.Precision.HIGHEST
    )
    dispatch = jnp.dot(slot_hot.T, token_hot).astype(jnp.bfloat16)
    outgoing = jnp.dot(dispatch, normed, preferred_element_type=jnp.float32).astype(jnp.bfloat16)
    outgoing = outgoing.reshape(devices, CAP, normed.shape[1])
    rows_in = lax.all_to_all(outgoing, "ep", split_axis=0, concat_axis=0, tiled=True)
    flat_rows = rows_in.reshape(-1, rows_in.shape[-1])
    both = jnp.dot(flat_rows, expert_gate_up[0], preferred_element_type=jnp.float32)
    active = (jax.nn.silu(both[:, :FFW]) * both[:, FFW:]).astype(jnp.bfloat16)
    result = jnp.dot(active, expert_down[0], preferred_element_type=jnp.float32).astype(
        jnp.bfloat16
    )
    returned = lax.all_to_all(
        result.reshape(rows_in.shape), "ep", split_axis=0, concat_axis=0, tiled=True
    )
    mixture = jnp.dot(
        mixing,
        returned.reshape(devices * CAP, normed.shape[1]).astype(jnp.float32),
        precision=lax.Precision.HIGHEST,
    )
    layer_out = (mid.astype(jnp.float32) + mixture).astype(jnp.bfloat16)
    return (layer_out, arrived_keys, arrived_values)


def solution(mesh):
    return jax.shard_map(
        on_device,
        mesh=mesh,
        in_specs=(
            P(("parts", "ep"), None),
            P(("parts", "ep"), None),
            P(("parts", "ep"), None),
            P(("parts", "ep"), None, None),
            P(("parts", "ep"), None, None),
            P(("parts", "ep"), None),
            P(("parts", "ep"), None),
            P(("parts", "ep"), None),
            P("ep", None),
            P(),
            P(("parts", "ep"), None),
            P(("parts", "ep"), None),
            P("ep", None, None),
            P("ep", None, None),
            P(("parts", "ep"), None),
            P(("parts", "ep"), None),
        ),
        out_specs=(
            P(("parts", "ep"), None),
            P(("parts", "ep"), None, None),
            P(("parts", "ep"), None, None),
        ),
        check_vma=False,
    )
```

profile of v0, /device:TPU:0, one launch (start us, length us, event | category | flops | bytes accessed | tf_op | source)
XLA Modules:
  0.0 368.1 jit_solution(4671859608133821340)
XLA Ops:
  7.9 0.7 iota_compare_fusion.8
  8.9 0.7 fusion.58
  9.7 3.5 gather_fusion
  13.4 21.8 %gather_fusion.1 = bf16[512,16,512]{2,1,0:T(8,128)(2,1)} fusion(bf16[256,16,512]{2,1,0:T(8,128)(2,1)} %param.19, s32[1024]{0:T(1024)S(1)} %pad_clamp_fusion.1), kind=kCustom, calls=%fused_computation.1 | custom fusion | bytes 16779264 | tf_op jit(solution)/shard_map/gather | solution.py:27
  35.3 12.6 %reshape.283 = bf16[32,256,4,128]{3,2,1,0:T(4,128)(2,1)} reshape(bf16[512,16,512]{2,1,0:T(8,128)(2,1)} %gather_fusion.1) | data formatting | bytes 16777216 | tf_op jit(solution)/shard_map/reshape | solution.py:27
  48.4 5.8 %bitcast_reduce_fusion = (f32[32,4,16]{2,1,0:T(4,128)S(1)}, f32[32,4,256,16]{2,3,1,0:T(8,128)S(1)}) fusion(pred[32,256]{1,0:T(8,128)(4,1)S(1)} %iota_compare_fusion.8, bf16[32,4,16,128]{3,2,1,0:T(8,128)(2,1)S(1)} %bitcast.90, bf16[32,256,4,128]{3,2,1,0:T(4,128)(2,1)} %reshape.283), kind=kOutput, calls=%fused_computation.18 | convolution fusion | flops 135788544 | bytes 11026432 | tf_op jit(solution)/shard_map/shgd,sthd->shgt/dot_general | solution.py:39
  54.3 1.0 fusion.13
  55.3 22.0 %gather_fusion.2 = bf16[512,16,512]{2,1,0:T(8,128)(2,1)} fusion(bf16[256,16,512]{2,1,0:T(8,128)(2,1)} %param.20, s32[1024]{0:T(1024)S(1)} %pad_clamp_fusion.1), kind=kCustom, calls=%fused_computation.2 | custom fusion | bytes 16779264 | tf_op jit(solution)/shard_map/gather | solution.py:30
  77.4 12.5 %reshape.286 = bf16[32,256,4,128]{3,2,1,0:T(4,128)(2,1)} reshape(bf16[512,16,512]{2,1,0:T(8,128)(2,1)} %gather_fusion.2) | data formatting | bytes 16777216 | tf_op jit(solution)/shard_map/reshape | solution.py:30
  89.9 4.7 %fusion.17 = bf16[32,4,16,128]{3,2,1,0:T(8,128)(2,1)S(1)} fusion(bf16[32,256,4,128]{3,2,1,0:T(4,128)(2,1)} %reshape.286, f32[32,4,256,16]{2,3,1,0:T(8,128)S(1)} %get-tuple-element.14, f32[32,4,16]{2,1,0:T(4,128)S(1)} %get-tuple-element.12, f32[32,4,16]{2,1,0:T(4,128)S(1)} %multiply_maximum_fusion, pred[32,256]{1,0:T(8,128)(4,1)S(1)} %iota_compare_fusion.8, ...), kind=kOutput, calls=%fused_computation.24 | convolution fusion | flops 137625600 | bytes 11108352 | tf_op jit(solution)/shard_map/shgt,sthd->shgd/dot_general | solution.py:60
  95.3 21.6 %all_to_all.36 = bf16[32,16,512]{2,0,1:T(8,128)(2,1)S(1)} all-to-all(bf16[32,16,512]{2,0,1:T(8,128)(2,1)S(1)} %copy.41), channel_id=1, replica_groups=mesh['parts'=2,'ep'=16] {'ep'}, dimensions={1} | all-to-all | bytes 1048576 | tf_op jit(solution)/shard_map/all_to_all | solution.py:115
  117.0 7.8 %fusion.64 = f32[512,4096]{1,0:T(8,128)} fusion(bf16[512,512]{1,0:T(8,128)(2,1)S(1)} %bitcast.85, bf16[512,4096]{1,0:T(8,128)(2,1)} %param.24), kind=kOutput, calls=%fused_computation.103 | convolution fusion | flops 2147483648 | bytes 13107200 | tf_op jit(solution)/shard_map/dot_general | solution.py:117
  126.6 102.3 %reduce-scatter.2.cloned.1.call-done = f32[32,4096]{1,0:T(8,128)} async-done(((f32[512,4096]{1,0:T(8,128)}), f32[32,4096]{1,0:T(8,128)}) %reduce-scatter.2.cloned.1.call-update) | async-done | bytes 524304 | tf_op jit(solution)/shard_map/reduce_scatter | solution.py:116
  228.9 1.2 fusion.26
  230.1 2.4 convolution_convert_fusion
  232.5 4.6 %all-to-all-start.1 = ((bf16[16,16,4096]{2,1,0:T(8,128)(2,1)}), bf16[16,16,4096]{2,1,0:T(8,128)(2,1)S(1)}, u32[]{:S(2)}, u32[]{:S(2)}) async-start(bf16[16,16,4096]{2,1,0:T(8,128)(2,1)} %bitcast.9), calls=%async_computation.2 | async-start | bytes 4194304 | tf_op jit(solution)/shard_map/all_to_all | solution.py:146
  237.2 2.8 gather_fusion.3
  240.0 2.8 gather_fusion.4
  243.0 0.9 copy.47
  244.1 0.9 copy.49
  245.0 33.3 %all-to-all-done.1 = bf16[16,16,4096]{2,1,0:T(8,128)(2,1)S(1)} async-done(((bf16[16,16,4096]{2,1,0:T(8,128)(2,1)}), bf16[16,16,4096]{2,1,0:T(8,128)(2,1)S(1)}, u32[]{:S(2)}, u32[]{:S(2)}) %all-to-all-start.1) | async-done | bytes 2097184 | tf_op jit(solution)/shard_map/all_to_all | solution.py:146
  278.3 11.2 %all-to-all-start.3 = ((bf16[16,16,512]{2,1,0:T(8,128)(2,1)}), bf16[16,16,512]{2,1,0:T(8,128)(2,1)S(1)}, u32[]{:S(2)}, u32[]{:S(2)}) async-start(bf16[16,16,512]{2,1,0:T(8,128)(2,1)} %copy.47), calls=%async_computation.4 | async-start | bytes 524288 | tf_op jit(solution)/shard_map/all_to_all | solution.py:103
  289.5 7.6 %fusion = f32[256,1536]{1,0:T(8,128)} fusion(bf16[256,4096]{1,0:T(8,128)(2,1)S(1)} %bitcast.86, bf16[1,4096,1536]{2,1,0:T(8,128)(2,1)} %param.28), kind=kOutput, calls=%fused_computation.5 | convolution fusion | flops 3221225472 | bytes 16252928 | tf_op jit(solution)/shard_map/dot_general | solution.py:148
  297.1 2.5 all-to-all-done.3
  299.5 3.5 all-to-all-start.4
  303.1 6.5 %fusion.8 = bf16[256,4096]{1,0:T(8,128)(2,1)} fusion(bf16[1,768,4096]{2,1,0:T(8,128)(2,1)} %param.29, f32[256,1536]{1,0:T(8,128)} %fusion), kind=kOutput, calls=%fused_computation.14 | convolution fusion | flops 1612840960 | bytes 9961472 | tf_op jit(solution)/shard_map/dot_general | solution.py:150
  309.6 3.6 all-to-all-done.4
  313.1 3.8 %all-to-all-start.2 = ((bf16[16,16,4096]{2,1,0:T(8,128)(2,1)}), bf16[16,16,4096]{2,1,0:T(8,128)(2,1)S(1)}, u32[]{:S(2)}, u32[]{:S(2)}) async-start(bf16[16,16,4096]{2,1,0:T(8,128)(2,1)} %bitcast.87), calls=%async_computation.3 | async-start | bytes 4194304 | tf_op jit(solution)/shard_map/all_to_all | solution.py:153
  317.6 40.5 %all-to-all-done.2 = bf16[16,16,4096]{2,1,0:T(8,128)(2,1)S(1)} async-done(((bf16[16,16,4096]{2,1,0:T(8,128)(2,1)}), bf16[16,16,4096]{2,1,0:T(8,128)(2,1)S(1)}, u32[]{:S(2)}, u32[]{:S(2)}) %all-to-all-start.2) | async-done | bytes 2097184 | tf_op jit(solution)/shard_map/all_to_all | solution.py:153
  358.0 1.8 fusion.11
  359.9 0.7 copy.71
  360.6 0.7 copy.72
  (61 shorter events, 5.5 us)
Async XLA Ops:
  7.2 2.6 copy-start
  7.2 221.7 %reduce-scatter.2.cloned.1.call-start = ((), (), s32[]{:S(2)}) async-start(), calls=%async_computation.6 | async-start | bytes 8912896 | tf_op jit(solution)/shard_map/reduce_scatter | solution.py:116
  35.3 12.6 %copy-start.2 = (bf16[32,8192]{1,0:T(8,128)(2,1)S(1)}, bf16[32,8192]{1,0:T(8,128)(2,1)}, u32[]{:S(2)}) copy-start(bf16[32,8192]{1,0:T(8,128)(2,1)} %param.16) | copy-start | bytes 1572868
  35.3 12.7 %copy-start.4 = (bf16[32,512]{1,0:T(8,128)(2,1)S(1)}, bf16[32,512]{1,0:T(8,128)(2,1)}, u32[]{:S(2)}) copy-start(bf16[32,512]{1,0:T(8,128)(2,1)} %param.17) | copy-start | bytes 98308
  77.4 12.6 %copy-start.5 = (bf16[32,512]{1,0:T(8,128)(2,1)S(1)}, bf16[32,512]{1,0:T(8,128)(2,1)}, u32[]{:S(2)}) copy-start(bf16[32,512]{1,0:T(8,128)(2,1)} %param.18) | copy-start | bytes 98308
  124.7 0.7 copy-start.7
  124.7 104.2 %copy-start.3 = (bf16[32,4096]{1,0:T(8,128)(2,1)S(1)}, bf16[32,4096]{1,0:T(8,128)(2,1)}, u32[]{:S(2)}) copy-start(bf16[32,4096]{1,0:T(8,128)(2,1)} %param.23) | copy-start | bytes 786436
  124.7 105.4 %copy-start.6 = (f32[4096]{0:T(1024)S(1)}, f32[4096]{0:T(1024)}, u32[]{:S(2)}) copy-start(f32[4096]{0:T(1024)} %param.25) | copy-start | bytes 49156
  232.5 4.6 %copy-start.10 = (s32[1,16]{1,0:T(1,128)S(1)}, s32[1,16]{1,0:T(1,128)}, u32[]{:S(2)}) copy-start(s32[1,16]{1,0:T(1,128)} %param.30) | copy-start | bytes 196
  232.5 10.2 %copy-start.9 = (s32[16,1]{0,1:T(1,128)S(1)}, s32[16,1]{0,1:T(1,128)}, u32[]{:S(2)}) copy-start(s32[16,1]{0,1:T(1,128)} %param.31) | copy-start | bytes 196
  232.5 45.7 %all-to-all-start.1 = ((bf16[16,16,4096]{2,1,0:T(8,128)(2,1)}), bf16[16,16,4096]{2,1,0:T(8,128)(2,1)S(1)}, u32[]{:S(2)}, u32[]{:S(2)}) async-start(bf16[16,16,4096]{2,1,0:T(8,128)(2,1)} %bitcast.9), calls=%async_computation.2 | async-start | bytes 4194304 | tf_op jit(solution)/shard_map/all_to_all | solution.py:146
  278.3 21.3 %all-to-all-start.3 = ((bf16[16,16,512]{2,1,0:T(8,128)(2,1)}), bf16[16,16,512]{2,1,0:T(8,128)(2,1)S(1)}, u32[]{:S(2)}, u32[]{:S(2)}) async-start(bf16[16,16,512]{2,1,0:T(8,128)(2,1)} %copy.47), calls=%async_computation.4 | async-start | bytes 524288 | tf_op jit(solution)/shard_map/all_to_all | solution.py:103
  299.5 13.6 %all-to-all-start.4 = ((bf16[16,16,512]{2,1,0:T(8,128)(2,1)}), bf16[16,16,512]{2,1,0:T(8,128)(2,1)S(1)}, u32[]{:S(2)}, u32[]{:S(2)}) async-start(bf16[16,16,512]{2,1,0:T(8,128)(2,1)} %copy.49), calls=%async_computation.5 | async-start | bytes 524288 | tf_op jit(solution)/shard_map/all_to_all | solution.py:104
  313.1 3.9 %copy-start.8 = (f32[32,8]{0,1:T(8,128)S(1)}, f32[32,8]{0,1:T(8,128)}, u32[]{:S(2)}) copy-start(f32[32,8]{0,1:T(8,128)} %param.27) | copy-start | bytes 3076
  313.1 44.9 %all-to-all-start.2 = ((bf16[16,16,4096]{2,1,0:T(8,128)(2,1)}), bf16[16,16,4096]{2,1,0:T(8,128)(2,1)S(1)}, u32[]{:S(2)}, u32[]{:S(2)}) async-start(bf16[16,16,4096]{2,1,0:T(8,128)(2,1)} %bitcast.87), calls=%async_computation.3 | async-start | bytes 4194304 | tf_op jit(solution)/shard_map/all_to_all | solution.py:153
  317.0 44.3 %copy-start.1 = (s32[1,256]{1,0:T(1,128)S(1)}, s32[1,256]{1,0:T(1,128)}, u32[]{:S(2)}) copy-start(s32[1,256]{1,0:T(1,128)} %param.22) | copy-start | bytes 3076
Sparse Core Ops, SparseCore 0:
  124.9 103.9 reduce-scatter.1
where the time goes:
time: 375 us; the launch traced here: 368 us
  waiting for transfers between devices  182 us (49%)
  local copies, waits for them, and re-layouts  83.5 us (22%)
  matrix products  37.8 us (10%)
  starting transfers between devices  23.3 us (6%)
  blocking collectives  21.6 us (6%)
  between operations  14.3 us (4%)
  other arithmetic  5.4 us (1%)
    reduce_scatter x1, waiting for transfers between devices, on_device(): lax.psum_scatter(jnp.dot(head_rows, out_weight, preferred_element_type=jn...  102 us
    all_to_all x1, waiting for transfers between devices, on_device(): lax.all_to_all(result.reshape(rows_in.shape), 'ep', split_axis=0, concat_...  40.5 us
    all_to_all x1, waiting for transfers between devices, on_device(): lax.all_to_all(outgoing, 'ep', split_axis=0, concat_axis=0, tiled=True)  33.3 us
    gather x1, local copies, waits for them, and re-layouts, attend_local(): pooled_values[physical_page]  22 us
    gather x1, local copies, waits for them, and re-layouts, attend_local(): pooled_keys[physical_page]  21.8 us
    all_to_all x1, blocking collectives, on_device(): lax.all_to_all(attended, 'ep', split_axis=1, concat_axis=0, tiled=True)  21.6 us
    reshape x1, local copies, waits for them, and re-layouts, attend_local(): pooled_keys[physical_page]  12.6 us
    reshape x1, local copies, waits for them, and re-layouts, attend_local(): pooled_values[physical_page]  12.5 us
  transfers between devices with their start and end apart: 5, of which 5 were waited for; matrix products, arithmetic and copies ran while one was open for 6% of the time, Pallas kernels for 0%

commit v1 on v0

v1 whole, which is shorter than its diff:
```python
import functools
import math

import jax
import jax.numpy as jnp
from jax import lax
from jax.experimental import pallas as pl
from jax.experimental.pallas import tpu as pltpu
from jax.sharding import PartitionSpec as P

QUERY_HEADS = 64
KEY_VALUE_HEADS = 4
HEAD_SIZE = 128
PAGE_TOKENS = 16
MOST_SEQ_PAGES = 16
SEQ_UNROLL = 4
PLANE = 4
MESH = pl.DeviceIdType.MESH


def attend_kernel(
    len_ref, order_ref, mig_page_ref, mig_dest_ref,
    q_ref, fk_ref, fv_ref, k_ref, v_ref,
    out_ref, mk_ref, mv_ref,
    ks, vs, fkf, fvf,
):
    pages = k_ref.shape[0]
    sequences = q_ref.shape[0]
    group = QUERY_HEADS // KEY_VALUE_HEADS
    width = KEY_VALUE_HEADS * HEAD_SIZE
    tokens = MOST_SEQ_PAGES * PAGE_TOKENS
    scale = 1.0 / math.sqrt(HEAD_SIZE)

    mk_ref[...] = jnp.zeros_like(mk_ref)
    mv_ref[...] = jnp.zeros_like(mv_ref)
    for i in range(mig_dest_ref.shape[0]):
        page, dest = mig_page_ref[0, i], mig_dest_ref[i, 0]
        mk_ref[dest] = k_ref[page]
        mv_ref[dest] = v_ref[page]

    fkf[...] = fk_ref[...].astype(jnp.float32)
    fvf[...] = fv_ref[...].astype(jnp.float32)
    row_head = lax.broadcasted_iota(jnp.int32, (QUERY_HEADS, width), 0) // group
    col_head = lax.broadcasted_iota(jnp.int32, (QUERY_HEADS, width), 1) // HEAD_SIZE
    diagonal = (row_head == col_head).astype(jnp.float32).astype(jnp.bfloat16)
    place = lax.broadcasted_iota(jnp.int32, (QUERY_HEADS, tokens), 1)

    def block(i, start):
        for u in range(SEQ_UNROLL):
            s = i * SEQ_UNROLL + u
            length = len_ref[0, s]
            for p in range(MOST_SEQ_PAGES):
                page = order_ref[0, jnp.minimum(start + p, pages - 1)]
                ks[u, p * PAGE_TOKENS:(p + 1) * PAGE_TOKENS, :] = k_ref[page]
                vs[u, p * PAGE_TOKENS:(p + 1) * PAGE_TOKENS, :] = v_ref[page]
            start = start + lax.div(length + (PAGE_TOKENS - 1), PAGE_TOKENS)
            q = q_ref[s]
            q_wide = jnp.concatenate([q] * KEY_VALUE_HEADS, axis=1) * diagonal
            scores = lax.dot_general(
                q_wide, ks[u], (((1,), (1,)), ((), ())), preferred_element_type=jnp.float32
            ) * scale
            scores = jnp.where(place < length, scores, -1e30)
            own = jnp.sum(
                q_wide.astype(jnp.float32) * fkf[pl.ds(s, 1), :], axis=1, keepdims=True
            ) * scale
            highest = jnp.maximum(jnp.max(scores, axis=1, keepdims=True), own)
            weights = jnp.exp(scores - highest)
            own_weight = jnp.exp(own - highest)
            total = jnp.sum(weights, axis=1, keepdims=True) + own_weight
            inverse = 1.0 / total
            probs = (weights * inverse).astype(jnp.bfloat16)
            own_prob = (own_weight * inverse).astype(jnp.bfloat16).astype(jnp.float32)
            mixed = jnp.dot(probs, vs[u], preferred_element_type=jnp.float32)
            mixed = mixed + own_prob * fvf[pl.ds(s, 1), :]
            out_ref[s] = jnp.concatenate(
                [
                    mixed[h * group:(h + 1) * group, h * HEAD_SIZE:(h + 1) * HEAD_SIZE]
                    for h in range(KEY_VALUE_HEADS)
                ],
                axis=0,
            ).astype(jnp.bfloat16)
        return start

    lax.fori_loop(0, sequences // SEQ_UNROLL, block, jnp.int32(0))


def attend(queries, fresh_keys, fresh_values, pooled_keys, pooled_values, lengths, page_order,
           mig_pages, mig_dest, n):
    sequences = queries.shape[0]
    width = KEY_VALUE_HEADS * HEAD_SIZE
    tokens = MOST_SEQ_PAGES * PAGE_TOKENS
    smem = pl.BlockSpec(memory_space=pltpu.SMEM)
    vmem = pl.BlockSpec(memory_space=pltpu.VMEM)
    page = (PAGE_TOKENS, width)
    return pl.pallas_call(
        attend_kernel,
        out_shape=(
            jax.ShapeDtypeStruct((sequences, QUERY_HEADS, HEAD_SIZE), jnp.bfloat16),
            jax.ShapeDtypeStruct((n,) + page, jnp.bfloat16),
            jax.ShapeDtypeStruct((n,) + page, jnp.bfloat16),
        ),
        in_specs=[smem] * 4 + [vmem] * 5,
        out_specs=(vmem,) * 3,
        scratch_shapes=[
            pltpu.VMEM((SEQ_UNROLL, tokens, width), jnp.bfloat16),
            pltpu.VMEM((SEQ_UNROLL, tokens, width), jnp.bfloat16),
            pltpu.VMEM((sequences, width), jnp.float32),
            pltpu.VMEM((sequences, width), jnp.float32),
        ],
        compiler_params=pltpu.CompilerParams(vmem_limit_bytes=40 * 1024 * 1024),
    )(lengths, page_order, mig_pages, mig_dest,
      queries.reshape(sequences, QUERY_HEADS, HEAD_SIZE), fresh_keys, fresh_values,
      pooled_keys, pooled_values)


def layer_kernel(
    n, attn_ref, gate_ref, hidden_ref, gain_ref, mk_ref, mv_ref, wo_hbm, wgu_hbm, wd_hbm,
    out_ref, ak_ref, av_ref,
    wo, wgu, wd, heads, gates, part, crecv, yrecv, zrecv, rows, act, mid, acc,
    wsem, asend, arecv, gsend, grecv, ksend, krecv, vsend, vrecv, rs, nsz, nsy, nsc, nrecv,
):
    G = n // PLANE
    me = lax.axis_index("ep")
    g = lax.div(me, PLANE)
    lane = lax.rem(me, PLANE)
    b = lax.div(lane, 2)
    c = lax.rem(lane, 2)
    S = hidden_ref.shape[0]
    D = hidden_ref.shape[1]
    FFW = wd_hbm.shape[0]
    block_rows = PLANE * S

    def dev(gg, bb, cc):
        return {"ep": gg * PLANE + bb * 2 + cc}

    def remote(src, dst, send, recv, to):
        return pltpu.make_async_remote_copy(
            src_ref=src, dst_ref=dst, send_sem=send, recv_sem=recv, device_id=to,
            device_id_type=MESH,
        )

    load_wo = pltpu.make_async_copy(wo_hbm, wo, wsem.at[0])
    load_wgu = pltpu.make_async_copy(wgu_hbm, wgu, wsem.at[1])
    load_wd = pltpu.make_async_copy(wd_hbm, wd, wsem.at[2])
    load_wo.start()
    load_wgu.start()
    load_wd.start()
    own_k = pltpu.make_async_copy(mk_ref.at[me], ak_ref.at[me], wsem.at[3])
    own_v = pltpu.make_async_copy(mv_ref.at[me], av_ref.at[me], wsem.at[4])
    own_k.start()
    own_v.start()
    heads[me] = attn_ref[me]
    gates[me] = gate_ref[...]

    barrier = pltpu.get_barrier_semaphore()

    @pl.loop(1, n)
    def _(i):
        pl.semaphore_signal(
            barrier, inc=1, device_id={"ep": lax.rem(me + i, n)}, device_id_type=MESH
        )

    pl.semaphore_wait(barrier, n - 1)

    def peer_of(k):
        i = lax.div(k, PLANE) + 1
        return lax.rem(g + (G - i), G) * PLANE + lax.rem(lane + 1 + lax.rem(k, PLANE), PLANE)

    def attn_copy(slot, peer):
        return remote(attn_ref.at[peer], heads.at[slot], asend.at[peer], arecv.at[slot],
                      {"ep": peer})

    def gate_copy(slot, peer):
        return remote(gate_ref, gates.at[slot], gsend.at[peer], grecv.at[slot], {"ep": peer})

    def key_copy(slot, peer):
        return remote(mk_ref.at[peer], ak_ref.at[slot], ksend.at[peer], krecv.at[slot],
                      {"ep": peer})

    def value_copy(slot, peer):
        return remote(mv_ref.at[peer], av_ref.at[slot], vsend.at[peer], vrecv.at[slot],
                      {"ep": peer})

    @pl.loop(0, n - 1)
    def _(k):
        attn_copy(me, peer_of(k)).start()

    @pl.loop(0, n - 1)
    def _(k):
        gate_copy(me, peer_of(k)).start()
        key_copy(me, peer_of(k)).start()
        value_copy(me, peer_of(k)).start()

    def c_copy(r, gi):
        return remote(part.at[gi, :, 1 - c], crecv.at[r, gi], rs.at[r, 0, gi], rs.at[r, 1, gi],
                      dev(g, b, 1 - c))

    def y_copy(r, gi):
        return remote(crecv.at[r, gi, 1 - b], yrecv.at[r, gi], rs.at[r, 2, gi], rs.at[r, 3, gi],
                      dev(g, 1 - b, c))

    def z_copy(r, gi, slot):
        return remote(yrecv.at[r, gi], zrecv.at[r, slot], rs.at[r, 4, gi], rs.at[r, 5, slot],
                      dev(gi, b, c))

    def core_stage(r, gi):
        c_copy(r, gi).wait_recv()
        for bb in range(2):
            crecv[r, gi, bb] = (
                part[gi, bb, c].astype(jnp.float32) + crecv[r, gi, bb].astype(jnp.float32)
            ).astype(jnp.bfloat16)
        y_copy(r, gi).start()

    def y_stage(r, gi):
        y_copy(r, gi).wait_recv()
        yrecv[r, gi] = (
            crecv[r, gi, b].astype(jnp.float32) + yrecv[r, gi].astype(jnp.float32)
        ).astype(jnp.bfloat16)

    def collect(r):
        acc[...] = yrecv[r, g].astype(jnp.float32)

        @pl.loop(1, G)
        def _(i):
            src = lax.rem(g + i, G)
            z_copy(r, g, src).wait_recv()
            acc[...] += zrecv[r, src].astype(jnp.float32)

    load_wo.wait()
    tile = 1024

    @pl.loop(0, G + 2)
    def _(t):
        @pl.when(t < G)
        def _():
            gi = lax.rem(g + 1 + t, G)
            for j in range(PLANE):
                src = gi * PLANE + j

                @pl.when(src != me)
                def _():
                    attn_copy(src, src).wait_recv()

            left = heads[pl.ds(gi * PLANE, PLANE)].reshape(block_rows, heads.shape[2])
            for j in range(D // tile):
                part[gi, :, :, :, j * tile:(j + 1) * tile] = jnp.dot(
                    left, wo[:, j * tile:(j + 1) * tile], preferred_element_type=jnp.float32
                ).astype(jnp.bfloat16).reshape(2, 2, S, tile)
            c_copy(0, gi).start()

        @pl.when((t >= 1) & (t <= G))
        def _():
            core_stage(0, lax.rem(g + t, G))

        @pl.when(t >= 2)
        def _():
            gi = lax.rem(g + t - 1, G)
            y_stage(0, gi)

            @pl.when(t <= G)
            def _():
                z_copy(0, gi, g).start()

    collect(0)
    middle = (hidden_ref[...].astype(jnp.float32) + acc[...]).astype(jnp.bfloat16)
    mid[...] = middle
    middle = middle.astype(jnp.float32)
    scale = lax.rsqrt(jnp.mean(middle * middle, axis=1, keepdims=True) + 1e-06)
    rows[g, b, c] = (middle * scale * gain_ref[...]).astype(jnp.bfloat16)

    def row_copy(gg, bb, cc, send, to):
        slot = rows.at[gg, bb, cc]
        return remote(slot, slot, send, nrecv.at[gg, bb, cc], to)

    def rows_to_z(target):
        return row_copy(g, b, c, nsz.at[target], dev(target, b, c))

    def rows_to_y(gg):
        return row_copy(gg, b, c, nsy.at[gg], dev(g, 1 - b, c))

    def rows_to_core(gg, bb):
        return row_copy(gg, bb, c, nsc.at[gg, bb], dev(g, b, 1 - c))

    def arrival(gg, bb, cc):
        return row_copy(gg, bb, cc, nsy.at[gg], dev(g, b, 1 - c))

    rows_to_core(g, b).start()
    rows_to_y(g).start()

    @pl.loop(1, G)
    def _(i):
        rows_to_z(lax.rem(g + (G - i), G)).start()

    @pl.loop(0, n - 1)
    def _(k):
        peer = peer_of(k)
        gate_copy(peer, peer).wait_recv()

    @pl.loop(0, G)
    def _(gi):
        c_copy(0, gi).wait_send()

    load_wgu.wait()
    load_wd.wait()
    half = 256

    @pl.loop(0, G + 2)
    def _(t):
        @pl.when(t + 1 < G)
        def _():
            gi = lax.rem(g + t + 1, G)
            arrival(gi, b, c).wait_recv()
            rows_to_y(gi).start()
            rows_to_core(gi, b).start()

        @pl.when(t < G)
        def _():
            gi = lax.rem(g + t, G)
            arrival(gi, 1 - b, c).wait_recv()
            rows_to_core(gi, 1 - b).start()
            arrival(gi, b, 1 - c).wait_recv()
            arrival(gi, 1 - b, 1 - c).wait_recv()

            @pl.loop(0, FFW // half)
            def _(j):
                left = rows[gi].reshape(block_rows, D)
                at = pl.multiple_of(j * half, half)
                gate = jnp.dot(left, wgu[:, pl.ds(at, half)], preferred_element_type=jnp.float32)
                up = jnp.dot(left, wgu[:, pl.ds(FFW + at, half)],
                             preferred_element_type=jnp.float32)
                act[:, pl.ds(at, half)] = (gate * jax.nn.sigmoid(gate) * up).astype(jnp.bfloat16)

            table = gates[pl.ds(gi * PLANE, PLANE)].reshape(block_rows, gates.shape[2])
            column = lax.broadcasted_iota(jnp.int32, table.shape, 1)
            chosen = jnp.sum(jnp.where(column == me, table, 0.0), axis=1, keepdims=True)
            for j in range(D // tile):
                y = jnp.dot(act[...], wd[:, j * tile:(j + 1) * tile],
                            preferred_element_type=jnp.float32)
                y = y.astype(jnp.bfloat16).astype(jnp.float32) * chosen
                part[gi, :, :, :, j * tile:(j + 1) * tile] = y.astype(jnp.bfloat16).reshape(
                    2, 2, S, tile
                )
            c_copy(1, gi).start()

        @pl.when((t >= 1) & (t <= G))
        def _():
            core_stage(1, lax.rem(g + t - 1, G))

        @pl.when(t >= 2)
        def _():
            gi = lax.rem(g + t - 2, G)
            y_stage(1, gi)

            @pl.when(t >= 3)
            def _():
                z_copy(1, gi, g).start()

    collect(1)
    out_ref[...] = (mid[...].astype(jnp.float32) + acc[...]).astype(jnp.bfloat16)

    own_k.wait()
    own_v.wait()

    @pl.loop(0, n - 1)
    def _(k):
        peer = peer_of(k)
        attn_copy(me, peer).wait_send()
        gate_copy(me, peer).wait_send()
        key_copy(me, peer).wait_send()
        value_copy(me, peer).wait_send()
        key_copy(peer, peer).wait_recv()
        value_copy(peer, peer).wait_recv()

    @pl.loop(0, G)
    def _(gi):
        c_copy(1, gi).wait_send()
        rows_to_y(gi).wait_send()
        rows_to_core(gi, 0).wait_send()
        rows_to_core(gi, 1).wait_send()
        for r in range(2):
            y_copy(r, gi).wait_send()

    @pl.loop(1, G)
    def _(i):
        gi = lax.rem(g + i, G)
        rows_to_z(gi).wait_send()
        for r in range(2):
            z_copy(r, gi, g).wait_send()


def layer(n, attn, gate, hidden, gain, mk, mv, wo, wgu, wd):
    G = n // PLANE
    S, D = hidden.shape
    FFW = wd.shape[0]
    vmem = pl.BlockSpec(memory_space=pltpu.VMEM)
    anywhere = pl.BlockSpec(memory_space=pl.ANY)
    bf16 = jnp.bfloat16
    dma = pltpu.SemaphoreType.DMA
    return pl.pallas_call(
        functools.partial(layer_kernel, n),
        out_shape=(
            jax.ShapeDtypeStruct(hidden.shape, bf16),
            jax.ShapeDtypeStruct(mk.shape, bf16),
            jax.ShapeDtypeStruct(mv.shape, bf16),
        ),
        in_specs=[vmem] * 4 + [anywhere] * 5,
        out_specs=(vmem, anywhere, anywhere),
        scratch_shapes=[
            pltpu.VMEM(wo.shape, bf16),
            pltpu.VMEM(wgu.shape, bf16),
            pltpu.VMEM(wd.shape, bf16),
            pltpu.VMEM(attn.shape, bf16),
            pltpu.VMEM((n,) + gate.shape, jnp.float32),
            pltpu.VMEM((G, 2, 2, S, D), bf16),
            pltpu.VMEM((2, G, 2, S, D), bf16),
            pltpu.VMEM((2, G, S, D), bf16),
            pltpu.VMEM((2, G, S, D), bf16),
            pltpu.VMEM((G, 2, 2, S, D), bf16),
            pltpu.VMEM((PLANE * S, FFW), bf16),
            pltpu.VMEM((S, D), bf16),
            pltpu.VMEM((S, D), jnp.float32),
            dma((5,)),
            dma((n,)), dma((n,)), dma((n,)), dma((n,)),
            dma((n,)), dma((n,)), dma((n,)), dma((n,)),
            dma((2, 6, G)),
            dma((G,)), dma((G,)), dma((G, 2)), dma((G, 2, 2)),
        ],
        compiler_params=pltpu.CompilerParams(
            collective_id=0, has_side_effects=True, vmem_limit_bytes=63 * 1024 * 1024
        ),
    )(attn, gate, hidden, gain, mk, mv, wo, wgu, wd)


def on_device(
    queries, fresh_token_keys, fresh_token_values, pooled_keys, pooled_values, lengths, page_order,
    hidden, out_weight, norm_gain, expert_ids, gate_weights, expert_gate_up, expert_down,
    mig_pages, mig_dest,
):
    n = lax.axis_size("ep")
    sequences = queries.shape[0]
    attended, mk, mv = attend(
        queries, fresh_token_keys, fresh_token_values, pooled_keys, pooled_values, lengths,
        page_order, mig_pages, mig_dest, n,
    )
    attended = attended.reshape(sequences, n, out_weight.shape[0]).transpose(1, 0, 2)
    lanes = jnp.arange(128, dtype=jnp.int32)
    gate = jnp.sum(
        jnp.where(expert_ids[:, :, None] == lanes, gate_weights[:, :, None], 0.0), axis=1
    )
    return layer(
        n, attended, gate, hidden, norm_gain[None, :], mk, mv, out_weight, expert_gate_up[0],
        expert_down[0],
    )


def solution(mesh):
    return jax.shard_map(
        on_device,
        mesh=mesh,
        in_specs=(
            P(("parts", "ep"), None),
            P(("parts", "ep"), None),
            P(("parts", "ep"), None),
            P(("parts", "ep"), None, None),
            P(("parts", "ep"), None, None),
            P(("parts", "ep"), None),
            P(("parts", "ep"), None),
            P(("parts", "ep"), None),
            P("ep", None),
            P(),
            P(("parts", "ep"), None),
            P(("parts", "ep"), None),
            P("ep", None, None),
            P("ep", None, None),
            P(("parts", "ep"), None),
            P(("parts", "ep"), None),
        ),
        out_specs=(
            P(("parts", "ep"), None),
            P(("parts", "ep"), None, None),
            P(("parts", "ep"), None, None),
        ),
        check_vma=False,
    )
```

time: 375 us -> 166 us (0.44); the launches traced: 368 us -> 164 us
  waiting for transfers between devices: 182 us -> 0 us
  Pallas kernels: 0 us -> 143 us
  local copies, waits for them, and re-layouts: 83.5 us -> 19.1 us
  matrix products: 37.8 us -> 0 us
  starting transfers between devices: 23.3 us -> 0 us
  blocking collectives: 21.6 us -> 0 us
  between operations: 14.3 us -> 0.68 us
  other arithmetic: 5.4 us -> 0.75 us
    pallas_call x0 -> x2, Pallas kernels: none -> 143 us  [the longest x1 127 us: layer(): pl.pallas_call(functools.partial(layer_kernel, n), out_shape=(jax.ShapeDt...]
    reduce_scatter x1 -> x0, waiting for transfers between devices: 102 us -> none  [on_device(): lax.psum_scatter(jnp.dot(head_rows, out_weight, preferred_element_type=jn...]
    all_to_all x4 -> x0, waiting for transfers between devices: 79.8 us -> none  [the longest x1 40.5 us: on_device(): lax.all_to_all(result.reshape(rows_in.shape), 'ep', split_axis=0, concat_...]
    gather x6 -> x0, local copies, waits for them, and re-layouts: 53 us -> none  [the longest x1 22 us: attend_local(): pooled_values[physical_page]]
    dot_general x11 -> x0, matrix products: 37.8 us -> none  [the longest x1 7.76 us: on_device(): jnp.dot(head_rows, out_weight, preferred_element_type=jnp.float32)]
    reshape x4 -> x2, local copies, waits for them, and re-layouts: 25.2 us -> 1.41 us  [on_device(): attended.reshape(sequences, n, out_weight.shape[0]).transpose(1, 0, 2)]
    all_to_all x4 -> x0, starting transfers between devices: 23.2 us -> none  [the longest x1 11.2 us: on_device(): lax.all_to_all(send_keys, 'ep', split_axis=0, concat_axis=0, tiled=True)]
    all_to_all x1 -> x0, blocking collectives: 21.6 us -> none  [on_device(): lax.all_to_all(attended, 'ep', split_axis=1, concat_axis=0, tiled=True)]
  transfers between devices with their start and end apart: 5 -> 0, of which waited for: 5 -> 0; matrix products, arithmetic and copies ran while one was open for 6% -> 0% of each run, Pallas kernels for 0% -> 0%
where the time goes in v1:
time: 166 us; the launch traced here: 164 us
  Pallas kernels  143 us (86%)
  local copies, waits for them, and re-layouts  19.1 us (12%)
    pallas_call x1, Pallas kernels, layer(): pl.pallas_call(functools.partial(layer_kernel, n), out_shape=(jax.ShapeDt...  127 us
    unnamed x25, local copies, waits for them, and re-layouts  17.7 us
    pallas_call x1, Pallas kernels, attend(): pl.pallas_call(attend_kernel, out_shape=(jax.ShapeDtypeStruct((sequences,...  16.7 us

profile of v1, /device:TPU:0, one launch (start us, length us, event | category | flops | bytes accessed | tf_op | source)
XLA Modules:
  0.0 163.9 jit_solution(11360857035112481790)
XLA Ops:
  0.6 0.7 copy.26.mig_dest_ref
  1.4 0.8 copy.28
  2.1 0.8 copy.29
  2.9 0.7 select_reduce_fusion.gate_ref
  3.6 1.2 copy.30
  4.8 0.0 copy-start
  4.8 2.2 %copy-done = bf16[256,16,512]{2,1,0:T(8,128)(2,1)S(1)} copy-done((bf16[256,16,512]{2,1,0:T(8,128)(2,1)S(1)}, bf16[256,16,512]{2,1,0:T(8,128)(2,1)}, u32[]{:S(2)}) %copy-start) | copy-done | bytes 4194328
  7.0 0.0 copy-start.1
  7.0 2.2 %copy-done.1 = bf16[256,16,512]{2,1,0:T(8,128)(2,1)S(1)} copy-done((bf16[256,16,512]{2,1,0:T(8,128)(2,1)S(1)}, bf16[256,16,512]{2,1,0:T(8,128)(2,1)}, u32[]{:S(2)}) %copy-start.1) | copy-done | bytes 4194328
  9.2 0.0 copy-start.4
  9.2 0.8 copy-done.4
  9.9 0.0 copy-start.5
  9.9 0.8 copy-done.5
  10.7 0.0 copy-start.6
  10.7 0.7 copy-done.6
  11.4 0.0 copy-start.7
  11.4 0.7 copy-done.7
  12.0 0.0 copy-start.8
  12.0 0.7 copy-done.8
  12.7 16.7 %shard_map.175 = (bf16[32,64,128]{2,1,0:T(8,128)(2,1)S(1)}, bf16[16,16,512]{2,1,0:T(8,128)(2,1)S(1)}, bf16[16,16,512]{2,1,0:T(8,128)(2,1)S(1)}) custom-call(s32[1,32]{1,0:T(1,128)S(1)} %copy-done.7, s32[1,256]{1,0:T(1,128)S(1)} %copy-done.6, s32[1,16]{1,0:T(1,128)S(1)} %copy-done.8, s32[16,1]{1,0:T(8,128)S(1)} %copy.26.mig_dest_ref, ...), custom_call_target="tpu_custom_call" | custom-call | tf_op jit(solution)/shard_map/pallas_call | solution.py:95
  29.4 0.0 copy-start.2
  29.4 0.7 copy-done.2
  30.1 0.0 copy-start.3
  30.1 0.7 copy-done.3
  30.8 0.3 reshape.15
  31.1 1.1 copy.32
  32.2 126.6 %shard_map.176 = (bf16[32,4096]{1,0:T(8,128)(2,1)}, bf16[16,16,512]{2,1,0:T(8,128)(2,1)}, bf16[16,16,512]{2,1,0:T(8,128)(2,1)}) custom-call(bf16[16,32,512]{2,1,0:T(8,128)(2,1)} %bitcast.11, f32[32,128]{1,0:T(8,128)} %select_reduce_fusion.gate_ref, bf16[32,4096]{1,0:T(8,128)(2,1)} %hidden_ref.1, f32[1,4096]{1,0:T(1,128)} %bitcast.13, ...), custom_call_target="tpu_custom_call" | custom-call | tf_op jit(solution)/shard_map/pallas_call | solution.py:399
  158.9 1.7 %copy.36 = bf16[32,4096]{1,0:T(8,128)(2,1)} copy(bf16[32,4096]{1,0:T(8,128)(2,1)} %get-tuple-element.12) | data formatting | bytes 524288
  160.5 1.7 %copy.37 = bf16[16,16,512]{2,1,0:T(8,128)(2,1)} copy(bf16[16,16,512]{2,1,0:T(8,128)(2,1)} %get-tuple-element.13) | data formatting | bytes 524288
  162.2 1.7 %copy.38 = bf16[16,16,512]{2,1,0:T(8,128)(2,1)} copy(bf16[16,16,512]{2,1,0:T(8,128)(2,1)} %get-tuple-element.14) | data formatting | bytes 524288
Async XLA Ops:
  4.8 2.2 %copy-start = (bf16[256,16,512]{2,1,0:T(8,128)(2,1)S(1)}, bf16[256,16,512]{2,1,0:T(8,128)(2,1)}, u32[]{:S(2)}) copy-start(bf16[256,16,512]{2,1,0:T(8,128)(2,1)} %k_ref.1) | copy-start | bytes 12582916
  7.0 2.2 %copy-start.1 = (bf16[256,16,512]{2,1,0:T(8,128)(2,1)S(1)}, bf16[256,16,512]{2,1,0:T(8,128)(2,1)}, u32[]{:S(2)}) copy-start(bf16[256,16,512]{2,1,0:T(8,128)(2,1)} %v_ref.1) | copy-start | bytes 12582916
  9.2 0.8 copy-start.4
  9.9 0.8 copy-start.5
  10.7 0.7 copy-start.6
  11.4 0.7 copy-start.7
  12.0 0.7 copy-start.8
  29.4 0.7 copy-start.2
  30.1 0.7 copy-start.3

commit v2 on v1

v2 whole, which is shorter than its diff:
```python
import functools
import math

import jax
import jax.numpy as jnp
from jax import lax
from jax.experimental import pallas as pl
from jax.experimental.pallas import tpu as pltpu
from jax.sharding import PartitionSpec as P

QUERY_HEADS = 64
KEY_VALUE_HEADS = 4
HEAD_SIZE = 128
PAGE_TOKENS = 16
MOST_SEQ_PAGES = 16
SEQ_UNROLL = 4
PLANE = 4
MESH = pl.DeviceIdType.MESH


def layer_kernel(
    n, len_ref, order_ref, mig_page_ref, mig_dest_ref, ids_ref, weights_ref,
    q_hbm, fk_hbm, fv_hbm, k_hbm, v_hbm, hidden_hbm, gain_hbm, wo_hbm, wgu_hbm, wd_hbm,
    out_ref, ak_ref, av_ref,
    wo, wgu, wd, heads, gates, part, crecv, yrecv, zrecv, rows, act, mid, acc,
    q_in, qs, attn_ref, ks, vs, fresh, fkf, fvf, mk_ref, mv_ref, gate_ref, hidden_ref, gain_ref,
    wsem, asend, arecv, gsend, grecv, ksend, krecv, vsend, vrecv, rs, nsz, nsy, nsc, nrecv,
):
    G = n // PLANE
    me = lax.axis_index("ep")
    g = lax.div(me, PLANE)
    lane = lax.rem(me, PLANE)
    b = lax.div(lane, 2)
    c = lax.rem(lane, 2)
    S = hidden_ref.shape[0]
    D = hidden_ref.shape[1]
    FFW = wd_hbm.shape[0]
    block_rows = PLANE * S

    def dev(gg, bb, cc):
        return {"ep": gg * PLANE + bb * 2 + cc}

    def remote(src, dst, send, recv, to):
        return pltpu.make_async_remote_copy(
            src_ref=src, dst_ref=dst, send_sem=send, recv_sem=recv, device_id=to,
            device_id_type=MESH,
        )

    pages = k_hbm.shape[0]
    width = KEY_VALUE_HEADS * HEAD_SIZE
    kpool = wgu.at[0:pages, :, 0:width]
    vpool = wgu.at[0:pages, :, width:2 * width]
    load_k = pltpu.make_async_copy(k_hbm, kpool, wsem.at[0])
    load_v = pltpu.make_async_copy(v_hbm, vpool, wsem.at[1])
    load_q = pltpu.make_async_copy(q_hbm, q_in, wsem.at[2])
    load_fk = pltpu.make_async_copy(fk_hbm, fresh.at[0], wsem.at[3])
    load_fv = pltpu.make_async_copy(fv_hbm, fresh.at[1], wsem.at[4])
    load_wo = pltpu.make_async_copy(wo_hbm, wo, wsem.at[5])
    load_wd = pltpu.make_async_copy(wd_hbm, wd, wsem.at[6])
    load_hidden = pltpu.make_async_copy(hidden_hbm, hidden_ref, wsem.at[7])
    load_gain = pltpu.make_async_copy(gain_hbm, gain_ref, wsem.at[8])
    load_wgu = pltpu.make_async_copy(wgu_hbm, wgu, wsem.at[9])
    own_k = pltpu.make_async_copy(mk_ref.at[me], ak_ref.at[me], wsem.at[10])
    own_v = pltpu.make_async_copy(mv_ref.at[me], av_ref.at[me], wsem.at[11])
    for load in (load_k, load_v, load_q, load_fk, load_fv, load_wo, load_wd, load_hidden,
                 load_gain):
        load.start()

    barrier = pltpu.get_barrier_semaphore()

    @pl.loop(1, n)
    def _(i):
        pl.semaphore_signal(
            barrier, inc=1, device_id={"ep": lax.rem(me + i, n)}, device_id_type=MESH
        )

    experts = lax.broadcasted_iota(jnp.int32, (128, S), 0)
    table = jnp.zeros((128, S), jnp.float32)
    for k in range(ids_ref.shape[0]):
        table = table + jnp.where(experts == ids_ref[k:k + 1, :], weights_ref[k:k + 1, :], 0.0)
    table = jnp.concatenate([table, jnp.zeros((128, 128 - S), jnp.float32)], axis=1)
    gate_ref[...] = table.T[0:S, :]
    gates[me] = gate_ref[...]

    def near(t):
        closest = jnp.minimum(g, G - 1 - g)
        away = lax.div(t + 1, 2)
        side = jnp.where(lax.rem(t, 2) == 1, g - away, g + away)
        rest = jnp.where(g + g <= G - 1, t, G - 1 - t)
        return jnp.where(t <= closest + closest, side, rest)

    def peer_of(k):
        plane = near(G - 1 - lax.div(k, PLANE))
        return plane * PLANE + lax.rem(lane + 1 + lax.rem(k, PLANE), PLANE)

    half_rows = S // 2

    def attn_copy(slot, peer, part_no):
        at = pl.ds(pl.multiple_of(part_no * half_rows, half_rows), half_rows)
        return remote(attn_ref.at[peer, at], heads.at[slot, at], asend.at[part_no, peer],
                      arecv.at[part_no, slot], {"ep": peer})

    def gate_copy(slot, peer):
        return remote(gate_ref, gates.at[slot], gsend.at[peer], grecv.at[slot], {"ep": peer})

    def key_copy(slot, peer):
        return remote(mk_ref.at[peer], ak_ref.at[slot], ksend.at[peer], krecv.at[slot],
                      {"ep": peer})

    def value_copy(slot, peer):
        return remote(mv_ref.at[peer], av_ref.at[slot], vsend.at[peer], vrecv.at[slot],
                      {"ep": peer})

    def stage_pages(dest):
        page, found = jnp.int32(0), jnp.int32(0)
        for i in range(mig_page_ref.shape[1]):
            same = mig_dest_ref[0, i] == dest
            page = jnp.where(same, mig_page_ref[0, i], page)
            found = jnp.where(same, 1, found)
        keep = jnp.full((PAGE_TOKENS, width), found, jnp.int32) == 1
        zero = jnp.zeros((PAGE_TOKENS, width), jnp.float32)
        for pool, staged in ((0, mk_ref), (width, mv_ref)):
            rows_of = wgu[page, :, pool:pool + width].astype(jnp.float32)
            staged[dest] = jnp.where(keep, rows_of, zero).astype(jnp.bfloat16)

    load_k.wait()
    load_v.wait()
    stage_pages(me)
    own_k.start()
    own_v.start()
    pl.semaphore_wait(barrier, n - 1)

    @pl.loop(0, n - 1)
    def _(k):
        peer = peer_of(k)
        stage_pages(peer)
        key_copy(me, peer).start()
        value_copy(me, peer).start()
        gate_copy(me, peer).start()

    load_q.wait()
    load_fk.wait()
    load_fv.wait()
    for h in range(QUERY_HEADS):
        qs[pl.ds(h, S, stride=QUERY_HEADS), :] = q_in[
            :, h * HEAD_SIZE:(h + 1) * HEAD_SIZE
        ].astype(jnp.float32)
    fkf[...] = fresh[0].astype(jnp.float32)
    fvf[...] = fresh[1].astype(jnp.float32)

    group = QUERY_HEADS // KEY_VALUE_HEADS
    tokens = MOST_SEQ_PAGES * PAGE_TOKENS
    score_scale = 1.0 / math.sqrt(HEAD_SIZE)
    row_head = lax.broadcasted_iota(jnp.int32, (QUERY_HEADS, width), 0) // group
    col_head = lax.broadcasted_iota(jnp.int32, (QUERY_HEADS, width), 1) // HEAD_SIZE
    diagonal = (row_head == col_head).astype(jnp.float32).astype(jnp.bfloat16)
    place = lax.broadcasted_iota(jnp.int32, (QUERY_HEADS, tokens), 1)

    def attend_some(part_no, i, start):
        for u in range(SEQ_UNROLL):
            s = part_no * half_rows + i * SEQ_UNROLL + u
            length = len_ref[0, s]
            for p in range(MOST_SEQ_PAGES):
                page = order_ref[0, jnp.minimum(start + p, pages - 1)]
                ks[u, p * PAGE_TOKENS:(p + 1) * PAGE_TOKENS, :] = wgu[page, :, 0:width]
                vs[u, p * PAGE_TOKENS:(p + 1) * PAGE_TOKENS, :] = wgu[page, :, width:2 * width]
            start = start + lax.div(length + (PAGE_TOKENS - 1), PAGE_TOKENS)
            s_rows = pl.ds(pl.multiple_of(s * QUERY_HEADS, QUERY_HEADS), QUERY_HEADS)
            q = qs[s_rows, :].astype(jnp.bfloat16)
            q_wide = jnp.concatenate([q] * KEY_VALUE_HEADS, axis=1) * diagonal
            scores = lax.dot_general(
                q_wide, ks[u], (((1,), (1,)), ((), ())), preferred_element_type=jnp.float32
            ) * score_scale
            scores = jnp.where(place < length, scores, -1e30)
            own = jnp.sum(
                q_wide.astype(jnp.float32) * fkf[pl.ds(s, 1), :], axis=1, keepdims=True
            ) * score_scale
            highest = jnp.maximum(jnp.max(scores, axis=1, keepdims=True), own)
            weights = jnp.exp(scores - highest)
            own_weight = jnp.exp(own - highest)
            total = jnp.sum(weights, axis=1, keepdims=True) + own_weight
            inverse = 1.0 / total
            probs = (weights * inverse).astype(jnp.bfloat16)
            own_prob = (own_weight * inverse).astype(jnp.bfloat16).astype(jnp.float32)
            mixed = jnp.dot(probs, vs[u], preferred_element_type=jnp.float32)
            mixed = mixed + own_prob * fvf[pl.ds(s, 1), :]
            qs[s_rows, :] = jnp.concatenate(
                [
                    mixed[h * group:(h + 1) * group, h * HEAD_SIZE:(h + 1) * HEAD_SIZE]
                    for h in range(KEY_VALUE_HEADS)
                ],
                axis=0,
            )
        return start

    some = half_rows // SEQ_UNROLL
    head_share = QUERY_HEADS // n

    def attend_half(part_no, start):
        start = lax.fori_loop(0, some, functools.partial(attend_some, part_no), start)
        at = pl.ds(pl.multiple_of(part_no * half_rows, half_rows), half_rows)
        first = part_no * (half_rows * QUERY_HEADS)
        for h in range(QUERY_HEADS):
            d, j = h // head_share, h % head_share
            attn_ref[d, at, j * HEAD_SIZE:(j + 1) * HEAD_SIZE] = qs[
                pl.ds(first + h, half_rows, stride=QUERY_HEADS), :
            ].astype(jnp.bfloat16)

        @pl.loop(0, n - 1)
        def _(k):
            attn_copy(me, peer_of(k), part_no).start()

        return start

    lax.fori_loop(0, 2, attend_half, jnp.int32(0))
    heads[me] = attn_ref[me]
    load_wgu.start()

    def c_copy(r, gi):
        return remote(part.at[gi, :, 1 - c], crecv.at[r, gi], rs.at[r, 0, gi], rs.at[r, 1, gi],
                      dev(g, b, 1 - c))

    def y_copy(r, gi):
        return remote(crecv.at[r, gi, 1 - b], yrecv.at[r, gi], rs.at[r, 2, gi], rs.at[r, 3, gi],
                      dev(g, 1 - b, c))

    def z_copy(r, gi, slot):
        return remote(yrecv.at[r, gi], zrecv.at[r, slot], rs.at[r, 4, gi], rs.at[r, 5, slot],
                      dev(gi, b, c))

    def core_stage(r, gi):
        c_copy(r, gi).wait_recv()
        for bb in range(2):
            crecv[r, gi, bb] = (
                part[gi, bb, c].astype(jnp.float32) + crecv[r, gi, bb].astype(jnp.float32)
            ).astype(jnp.bfloat16)
        y_copy(r, gi).start()

    def y_stage(r, gi):
        y_copy(r, gi).wait_recv()
        yrecv[r, gi] = (
            crecv[r, gi, b].astype(jnp.float32) + yrecv[r, gi].astype(jnp.float32)
        ).astype(jnp.bfloat16)

    def collect(r):
        acc[...] = yrecv[r, g].astype(jnp.float32)

        @pl.loop(1, G)
        def _(i):
            src = lax.rem(g + i, G)
            z_copy(r, g, src).wait_recv()
            acc[...] += zrecv[r, src].astype(jnp.float32)

    load_wo.wait()
    tile = 1024

    @pl.loop(0, G + 2)
    def _(t):
        @pl.when(t < G)
        def _():
            gi = near(G - 1 - t)
            for j in range(PLANE):
                src = gi * PLANE + j

                @pl.when(src != me)
                def _():
                    attn_copy(src, src, 0).wait_recv()
                    attn_copy(src, src, 1).wait_recv()

            left = heads[pl.ds(gi * PLANE, PLANE)].reshape(block_rows, heads.shape[2])
            for j in range(D // tile):
                part[gi, :, :, :, j * tile:(j + 1) * tile] = jnp.dot(
                    left, wo[:, j * tile:(j + 1) * tile], preferred_element_type=jnp.float32
                ).astype(jnp.bfloat16).reshape(2, 2, S, tile)
            c_copy(0, gi).start()

        @pl.when((t >= 1) & (t <= G))
        def _():
            core_stage(0, near(G - t))

        @pl.when(t >= 2)
        def _():
            gi = near(G + 1 - t)
            y_stage(0, gi)

            @pl.when(t <= G)
            def _():
                z_copy(0, gi, g).start()

    collect(0)
    load_hidden.wait()
    load_gain.wait()
    middle = (hidden_ref[...].astype(jnp.float32) + acc[...]).astype(jnp.bfloat16)
    mid[...] = middle
    middle = middle.astype(jnp.float32)
    scale = lax.rsqrt(jnp.mean(middle * middle, axis=1, keepdims=True) + 1e-06)
    rows[g, b, c] = (middle * scale * gain_ref[...]).astype(jnp.bfloat16)

    def row_copy(gg, bb, cc, send, to):
        slot = rows.at[gg, bb, cc]
        return remote(slot, slot, send, nrecv.at[gg, bb, cc], to)

    def rows_to_z(gg, step):
        return row_copy(gg, b, c, nsz.at[gg, (step + 1) // 2], dev(g + step, b, c))

    def pass_on(gg, act_on):
        @pl.when((gg <= g) & (g + 1 < G))
        def _():
            act_on(rows_to_z(gg, 1))

        @pl.when((gg >= g) & (g >= 1))
        def _():
            act_on(rows_to_z(gg, -1))

    def rows_to_y(gg):
        return row_copy(gg, b, c, nsy.at[gg], dev(g, 1 - b, c))

    def rows_to_core(gg, bb):
        return row_copy(gg, bb, c, nsc.at[gg, bb], dev(g, b, 1 - c))

    def arrival(gg, bb, cc):
        return row_copy(gg, bb, cc, nsy.at[gg], dev(g, b, 1 - c))

    rows_to_core(g, b).start()
    rows_to_y(g).start()

    pass_on(g, lambda copy: copy.start())

    @pl.loop(0, n - 1)
    def _(k):
        peer = peer_of(k)
        gate_copy(peer, peer).wait_recv()

    @pl.loop(0, G)
    def _(gi):
        c_copy(0, gi).wait_send()

    load_wgu.wait()
    load_wd.wait()
    half = 256

    @pl.loop(0, G + 2)
    def _(t):
        @pl.when(t + 1 < G)
        def _():
            gi = near(t + 1)
            arrival(gi, b, c).wait_recv()
            pass_on(gi, lambda copy: copy.start())
            rows_to_y(gi).start()
            rows_to_core(gi, b).start()

        @pl.when(t < G)
        def _():
            gi = near(t)
            arrival(gi, 1 - b, c).wait_recv()
            rows_to_core(gi, 1 - b).start()
            arrival(gi, b, 1 - c).wait_recv()
            arrival(gi, 1 - b, 1 - c).wait_recv()

            @pl.loop(0, FFW // half)
            def _(j):
                left = rows[gi].reshape(block_rows, D)
                at = pl.multiple_of(j * half, half)
                gate = jnp.dot(left, wgu[:, :, pl.ds(at, half)].reshape(D, half),
                               preferred_element_type=jnp.float32)
                up = jnp.dot(left, wgu[:, :, pl.ds(FFW + at, half)].reshape(D, half),
                             preferred_element_type=jnp.float32)
                act[:, pl.ds(at, half)] = (gate * jax.nn.sigmoid(gate) * up).astype(jnp.bfloat16)

            table = gates[pl.ds(gi * PLANE, PLANE)].reshape(block_rows, gates.shape[2])
            column = lax.broadcasted_iota(jnp.int32, table.shape, 1)
            chosen = jnp.sum(jnp.where(column == me, table, 0.0), axis=1, keepdims=True)
            for j in range(D // tile):
                y = jnp.dot(act[...], wd[:, j * tile:(j + 1) * tile],
                            preferred_element_type=jnp.float32)
                y = y.astype(jnp.bfloat16).astype(jnp.float32) * chosen
                part[gi, :, :, :, j * tile:(j + 1) * tile] = y.astype(jnp.bfloat16).reshape(
                    2, 2, S, tile
                )
            c_copy(1, gi).start()

        @pl.when((t >= 1) & (t <= G))
        def _():
            core_stage(1, near(t - 1))

        @pl.when(t >= 2)
        def _():
            gi = near(t - 2)
            y_stage(1, gi)

            @pl.when(t >= 3)
            def _():
                z_copy(1, gi, g).start()

    collect(1)
    out_ref[...] = (mid[...].astype(jnp.float32) + acc[...]).astype(jnp.bfloat16)

    own_k.wait()
    own_v.wait()

    @pl.loop(0, n - 1)
    def _(k):
        peer = peer_of(k)
        attn_copy(me, peer, 0).wait_send()
        attn_copy(me, peer, 1).wait_send()
        gate_copy(me, peer).wait_send()
        key_copy(me, peer).wait_send()
        value_copy(me, peer).wait_send()
        key_copy(peer, peer).wait_recv()
        value_copy(peer, peer).wait_recv()

    @pl.loop(0, G)
    def _(gi):
        c_copy(1, gi).wait_send()
        rows_to_y(gi).wait_send()
        rows_to_core(gi, 0).wait_send()
        rows_to_core(gi, 1).wait_send()
        pass_on(gi, lambda copy: copy.wait_send())
        for r in range(2):
            y_copy(r, gi).wait_send()

    @pl.loop(1, G)
    def _(i):
        gi = lax.rem(g + i, G)
        for r in range(2):
            z_copy(r, gi, g).wait_send()


def layer(n, lengths, page_order, mig_pages, mig_dest, ids, weights, queries, fresh_keys,
          fresh_values, keys, values, hidden, gain, wo, wgu, wd):
    G = n // PLANE
    S, D = hidden.shape
    FFW = wd.shape[0]
    width = KEY_VALUE_HEADS * HEAD_SIZE
    tokens = MOST_SEQ_PAGES * PAGE_TOKENS
    pages = (n, PAGE_TOKENS, width)
    smem = pl.BlockSpec(memory_space=pltpu.SMEM)
    vmem = pl.BlockSpec(memory_space=pltpu.VMEM)
    anywhere = pl.BlockSpec(memory_space=pl.ANY)
    bf16 = jnp.bfloat16
    dma = pltpu.SemaphoreType.DMA
    return pl.pallas_call(
        functools.partial(layer_kernel, n),
        out_shape=(
            jax.ShapeDtypeStruct(hidden.shape, bf16),
            jax.ShapeDtypeStruct(pages, bf16),
            jax.ShapeDtypeStruct(pages, bf16),
        ),
        in_specs=[smem] * 4 + [vmem] * 2 + [anywhere] * 10,
        out_specs=(vmem, anywhere, anywhere),
        scratch_shapes=[
            pltpu.VMEM(wo.shape, bf16),
            pltpu.VMEM(wgu.shape, bf16),
            pltpu.VMEM(wd.shape, bf16),
            pltpu.VMEM((n, S, wo.shape[0]), bf16),
            pltpu.VMEM((n, S, 128), jnp.float32),
            pltpu.VMEM((G, 2, 2, S, D), bf16),
            pltpu.VMEM((2, G, 2, S, D), bf16),
            pltpu.VMEM((2, G, S, D), bf16),
            pltpu.VMEM((2, G, S, D), bf16),
            pltpu.VMEM((G, 2, 2, S, D), bf16),
            pltpu.VMEM((PLANE * S, FFW), bf16),
            pltpu.VMEM((S, D), bf16),
            pltpu.VMEM((S, D), jnp.float32),
            pltpu.VMEM(queries.shape, bf16),
            pltpu.VMEM((S * QUERY_HEADS, HEAD_SIZE), jnp.float32),
            pltpu.VMEM((n, S, wo.shape[0]), bf16),
            pltpu.VMEM((SEQ_UNROLL, tokens, width), bf16),
            pltpu.VMEM((SEQ_UNROLL, tokens, width), bf16),
            pltpu.VMEM((2, S, width), bf16),
            pltpu.VMEM((S, width), jnp.float32),
            pltpu.VMEM((S, width), jnp.float32),
            pltpu.VMEM(pages, bf16),
            pltpu.VMEM(pages, bf16),
            pltpu.VMEM((S, 128), jnp.float32),
            pltpu.VMEM(hidden.shape, bf16),
            pltpu.VMEM(gain.shape, jnp.float32),
            dma((12,)),
            dma((2, n)), dma((2, n)), dma((n,)), dma((n,)),
            dma((n,)), dma((n,)), dma((n,)), dma((n,)),
            dma((2, 6, G)),
            dma((G, 2)), dma((G,)), dma((G, 2)), dma((G, 2, 2)),
        ],
        compiler_params=pltpu.CompilerParams(
            collective_id=0, has_side_effects=True, vmem_limit_bytes=63 * 1024 * 1024
        ),
    )(lengths, page_order, mig_pages, mig_dest, ids, weights, queries, fresh_keys, fresh_values,
      keys, values, hidden, gain, wo, wgu, wd)


def hand_out_kernel(a_ref, b_ref, c_ref, x_ref, y_ref, z_ref, sem):
    copies = [
        pltpu.make_async_copy(source, target, sem.at[i])
        for i, (source, target) in enumerate(((a_ref, x_ref), (b_ref, y_ref), (c_ref, z_ref)))
    ]
    for copy in copies:
        copy.start()
    for copy in copies:
        copy.wait()


def hand_out(*results):
    anywhere = pl.BlockSpec(memory_space=pl.ANY)
    return pl.pallas_call(
        hand_out_kernel,
        out_shape=tuple(jax.ShapeDtypeStruct(r.shape, r.dtype) for r in results),
        in_specs=[anywhere] * 3,
        out_specs=(anywhere,) * 3,
        scratch_shapes=[pltpu.SemaphoreType.DMA((3,))],
    )(*results)


def on_device(
    queries, fresh_token_keys, fresh_token_values, pooled_keys, pooled_values, lengths, page_order,
    hidden, out_weight, norm_gain, expert_ids, gate_weights, expert_gate_up, expert_down,
    mig_pages, mig_dest,
):
    n = lax.axis_size("ep")
    return hand_out(*layer(
        n, lengths, page_order, mig_pages, mig_dest.T, expert_ids.T, gate_weights.T, queries,
        fresh_token_keys, fresh_token_values, pooled_keys,
        pooled_values, hidden, norm_gain[None, :], out_weight,
        expert_gate_up.reshape(-1, PAGE_TOKENS, expert_gate_up.shape[2]), expert_down[0],
    ))


def solution(mesh):
    return jax.shard_map(
        on_device,
        mesh=mesh,
        in_specs=(
            P(("parts", "ep"), None),
            P(("parts", "ep"), None),
            P(("parts", "ep"), None),
            P(("parts", "ep"), None, None),
            P(("parts", "ep"), None, None),
            P(("parts", "ep"), None),
            P(("parts", "ep"), None),
            P(("parts", "ep"), None),
            P("ep", None),
            P(),
            P(("parts", "ep"), None),
            P(("parts", "ep"), None),
            P("ep", None, None),
            P("ep", None, None),
            P(("parts", "ep"), None),
            P(("parts", "ep"), None),
        ),
        out_specs=(
            P(("parts", "ep"), None),
            P(("parts", "ep"), None, None),
            P(("parts", "ep"), None, None),
        ),
        check_vma=False,
    )
```

time: 166 us -> 163 us (0.982); the launches traced: 164 us -> 163 us
  local copies, waits for them, and re-layouts: 19.1 us -> 0 us
  Pallas kernels: 143 us -> 162 us
    unnamed x25 -> x0, local copies, waits for them, and re-layouts: 17.7 us -> none
    pallas_call x1, Pallas kernels: 127 us -> 137 us  [layer(): pl.pallas_call(functools.partial(layer_kernel, n), out_shape=(jax.ShapeDt...]
    pallas_call x1, Pallas kernels: 16.7 us -> 25 us  [hand_out(): pl.pallas_call(hand_out_kernel, out_shape=tuple((jax.ShapeDtypeStruct(r.s...]
where the time goes in v2:
time: 163 us
  Pallas kernels  162 us (99%)
    pallas_call x1, Pallas kernels, layer(): pl.pallas_call(functools.partial(layer_kernel, n), out_shape=(jax.ShapeDt...  137 us
    pallas_call x1, Pallas kernels, hand_out(): pl.pallas_call(hand_out_kernel, out_shape=tuple((jax.ShapeDtypeStruct(r.s...  25 us

profile of v2, /device:TPU:0, one launch (start us, length us, event | category | flops | bytes accessed | tf_op | source)
XLA Modules:
  0.0 162.8 jit_solution(5213275171516544461)
XLA Ops:
  0.6 137.2 %shard_map.175 = (bf16[32,4096]{1,0:T(8,128)(2,1)}, bf16[16,16,512]{2,1,0:T(8,128)(2,1)}, bf16[16,16,512]{2,1,0:T(8,128)(2,1)}) custom-call(s32[1,32]{1,0:T(1,128)} %len_ref.1, s32[1,256]{1,0:T(1,128)} %order_ref.1, s32[1,16]{1,0:T(1,128)} %mig_page_ref.1, s32[1,16]{1,0:T(1,128)} %bitcast.11, s32[8,32]{1,0:T(8,128)} %bitcast.9, f32[8,32]{1,0:T(8,128)} %bitcast.10, ...), custom_call_target="tpu_custom_call" | custom-call | tf_op jit(solution)/shard_map/pallas_call | solution.py:442
  137.9 25.0 %shard_map.176 = (bf16[32,4096]{1,0:T(8,128)(2,1)}, bf16[16,16,512]{2,1,0:T(8,128)(2,1)}, bf16[16,16,512]{2,1,0:T(8,128)(2,1)}) custom-call(bf16[32,4096]{1,0:T(8,128)(2,1)} %get-tuple-element.6.a_ref, bf16[16,16,512]{2,1,0:T(8,128)(2,1)} %get-tuple-element.7.b_ref, bf16[16,16,512]{2,1,0:T(8,128)(2,1)} %get-tuple-element.8.c_ref), custom_call_target="tpu_custom_call" | custom-call | tf_op jit(solution)/shard_map/pallas_call | solution.py:504

commit v3 on v2

--- a/solution.py
+++ b/solution.py
@@ -62,7 +62,7 @@
     load_wgu = pltpu.make_async_copy(wgu_hbm, wgu, wsem.at[9])
     own_k = pltpu.make_async_copy(mk_ref.at[me], ak_ref.at[me], wsem.at[10])
     own_v = pltpu.make_async_copy(mv_ref.at[me], av_ref.at[me], wsem.at[11])
-    for load in (load_k, load_v, load_q, load_fk, load_fv, load_wo, load_wd, load_hidden,
+    for load in (load_q, load_fk, load_fv, load_k, load_v, load_wo, load_wd, load_hidden,
                  load_gain):
         load.start()
 
@@ -123,21 +123,6 @@
             rows_of = wgu[page, :, pool:pool + width].astype(jnp.float32)
             staged[dest] = jnp.where(keep, rows_of, zero).astype(jnp.bfloat16)
 
-    load_k.wait()
-    load_v.wait()
-    stage_pages(me)
-    own_k.start()
-    own_v.start()
-    pl.semaphore_wait(barrier, n - 1)
-
-    @pl.loop(0, n - 1)
-    def _(k):
-        peer = peer_of(k)
-        stage_pages(peer)
-        key_copy(me, peer).start()
-        value_copy(me, peer).start()
-        gate_copy(me, peer).start()
-
     load_q.wait()
     load_fk.wait()
     load_fv.wait()
@@ -148,6 +133,21 @@
     fkf[...] = fresh[0].astype(jnp.float32)
     fvf[...] = fresh[1].astype(jnp.float32)
 
+    load_k.wait()
+    load_v.wait()
+    stage_pages(me)
+    own_k.start()
+    own_v.start()
+    pl.semaphore_wait(barrier, n - 1)
+
+    @pl.loop(0, n - 1)
+    def _(k):
+        peer = peer_of(k)
+        stage_pages(peer)
+        key_copy(me, peer).start()
+        value_copy(me, peer).start()
+        gate_copy(me, peer).start()
+
     group = QUERY_HEADS // KEY_VALUE_HEADS
     tokens = MOST_SEQ_PAGES * PAGE_TOKENS
     score_scale = 1.0 / math.sqrt(HEAD_SIZE)
@@ -157,40 +157,51 @@
     place = lax.broadcasted_iota(jnp.int32, (QUERY_HEADS, tokens), 1)
 
     def attend_some(part_no, i, start):
-        for u in range(SEQ_UNROLL):
-            s = part_no * half_rows + i * SEQ_UNROLL + u
-            length = len_ref[0, s]
+        first = part_no * half_rows + i * SEQ_UNROLL
+        several = range(SEQ_UNROLL)
+        spans, lengths, q_wides, scores, owns, probs, own_probs, results = ([] for _ in range(8))
+        for u in several:
+            s = first + u
+            lengths.append(len_ref[0, s])
             for p in range(MOST_SEQ_PAGES):
                 page = order_ref[0, jnp.minimum(start + p, pages - 1)]
                 ks[u, p * PAGE_TOKENS:(p + 1) * PAGE_TOKENS, :] = wgu[page, :, 0:width]
                 vs[u, p * PAGE_TOKENS:(p + 1) * PAGE_TOKENS, :] = wgu[page, :, width:2 * width]
-            start = start + lax.div(length + (PAGE_TOKENS - 1), PAGE_TOKENS)
-            s_rows = pl.ds(pl.multiple_of(s * QUERY_HEADS, QUERY_HEADS), QUERY_HEADS)
-            q = qs[s_rows, :].astype(jnp.bfloat16)
-            q_wide = jnp.concatenate([q] * KEY_VALUE_HEADS, axis=1) * diagonal
-            scores = lax.dot_general(
-                q_wide, ks[u], (((1,), (1,)), ((), ())), preferred_element_type=jnp.float32
-            ) * score_scale
-            scores = jnp.where(place < length, scores, -1e30)
-            own = jnp.sum(
-                q_wide.astype(jnp.float32) * fkf[pl.ds(s, 1), :], axis=1, keepdims=True
-            ) * score_scale
-            highest = jnp.maximum(jnp.max(scores, axis=1, keepdims=True), own)
-            weights = jnp.exp(scores - highest)
-            own_weight = jnp.exp(own - highest)
-            total = jnp.sum(weights, axis=1, keepdims=True) + own_weight
-            inverse = 1.0 / total
-            probs = (weights * inverse).astype(jnp.bfloat16)
-            own_prob = (own_weight * inverse).astype(jnp.bfloat16).astype(jnp.float32)
-            mixed = jnp.dot(probs, vs[u], preferred_element_type=jnp.float32)
-            mixed = mixed + own_prob * fvf[pl.ds(s, 1), :]
-            qs[s_rows, :] = jnp.concatenate(
+            start = start + lax.div(lengths[u] + (PAGE_TOKENS - 1), PAGE_TOKENS)
+            spans.append(pl.ds(pl.multiple_of(s * QUERY_HEADS, QUERY_HEADS), QUERY_HEADS))
+            q = qs[spans[u], :].astype(jnp.bfloat16)
+            q_wides.append(jnp.concatenate([q] * KEY_VALUE_HEADS, axis=1) * diagonal)
+        for u in several:
+            scores.append(lax.dot_general(
+                q_wides[u], ks[u], (((1,), (1,)), ((), ())), preferred_element_type=jnp.float32
+            ) * score_scale)
+        for u in several:
+            owns.append(jnp.sum(
+                q_wides[u].astype(jnp.float32) * fkf[pl.ds(first + u, 1), :], axis=1,
+                keepdims=True,
+            ) * score_scale)
+        for u in several:
+            masked = jnp.where(place < lengths[u], scores[u], -1e30)
+            highest = jnp.maximum(jnp.max(masked, axis=1, keepdims=True), owns[u])
+            weights = jnp.exp(masked - highest)
+            own_weight = jnp.exp(owns[u] - highest)
+            inverse = 1.0 / (jnp.sum(weights, axis=1, keepdims=True) + own_weight)
+            probs.append((weights * inverse).astype(jnp.bfloat16))
+            own_probs.append((own_weight * inverse).astype(jnp.bfloat16).astype(jnp.float32))
+        for u in several:
+            mixed = jnp.dot(probs[u], vs[u], preferred_element_type=jnp.float32)
+            fresh_value = fvf[pl.ds(first + u, 1), :]
+            results.append(jnp.concatenate(
                 [
                     mixed[h * group:(h + 1) * group, h * HEAD_SIZE:(h + 1) * HEAD_SIZE]
+                    + own_probs[u][h * group:(h + 1) * group]
+                    * fresh_value[:, h * HEAD_SIZE:(h + 1) * HEAD_SIZE]
                     for h in range(KEY_VALUE_HEADS)
                 ],
                 axis=0,
-            )
+            ))
+        for u in several:
+            qs[spans[u], :] = results[u]
         return start
 
     some = half_rows // SEQ_UNROLL
@@ -339,19 +350,28 @@
     load_wd.wait()
     half = 256
 
+    def take_along_z(gi):
+        arrival(gi, b, c).wait_recv()
+        pass_on(gi, lambda copy: copy.start())
+        rows_to_y(gi).start()
+        rows_to_core(gi, b).start()
+
+    def turn(t):
+        return near(lax.rem(t + 1, G))
+
     @pl.loop(0, G + 2)
     def _(t):
-        @pl.when(t + 1 < G)
-        def _():
-            gi = near(t + 1)
-            arrival(gi, b, c).wait_recv()
-            pass_on(gi, lambda copy: copy.start())
-            rows_to_y(gi).start()
-            rows_to_core(gi, b).start()
+        @pl.when((t == 0) & (G > 1))
+        def _():
+            take_along_z(near(1))
+
+        @pl.when(t + 2 < G)
+        def _():
+            take_along_z(near(t + 2))
 
         @pl.when(t < G)
         def _():
-            gi = near(t)
+            gi = turn(t)
             arrival(gi, 1 - b, c).wait_recv()
             rows_to_core(gi, 1 - b).start()
             arrival(gi, b, 1 - c).wait_recv()
@@ -381,14 +401,14 @@
 
         @pl.when((t >= 1) & (t <= G))
         def _():
-            core_stage(1, near(t - 1))
+            core_stage(1, turn(t - 1))
 
         @pl.when(t >= 2)
         def _():
-            gi = near(t - 2)
+            gi = turn(t - 2)
             y_stage(1, gi)
 
-            @pl.when(t >= 3)
+            @pl.when(t <= G)
             def _():
                 z_copy(1, gi, g).start()
 
@@ -488,15 +508,19 @@
       keys, values, hidden, gain, wo, wgu, wd)
 
 
-def hand_out_kernel(a_ref, b_ref, c_ref, x_ref, y_ref, z_ref, sem):
-    copies = [
-        pltpu.make_async_copy(source, target, sem.at[i])
-        for i, (source, target) in enumerate(((a_ref, x_ref), (b_ref, y_ref), (c_ref, z_ref)))
-    ]
-    for copy in copies:
-        copy.start()
-    for copy in copies:
-        copy.wait()
+def hand_out_kernel(a_ref, b_ref, c_ref, x_ref, y_ref, z_ref, a_held, b_held, c_held, sem):
+    moves = (
+        (a_ref, a_held, x_ref), (b_ref, b_held, y_ref), (c_ref, c_held, z_ref)
+    )
+    loads = [pltpu.make_async_copy(s, h, sem.at[0, i]) for i, (s, h, _) in enumerate(moves)]
+    stores = [pltpu.make_async_copy(h, t, sem.at[1, i]) for i, (_, h, t) in enumerate(moves)]
+    for load in loads:
+        load.start()
+    for load, store in zip(loads, stores):
+        load.wait()
+        store.start()
+    for store in stores:
+        store.wait()
 
 
 def hand_out(*results):
@@ -506,7 +530,8 @@
         out_shape=tuple(jax.ShapeDtypeStruct(r.shape, r.dtype) for r in results),
         in_specs=[anywhere] * 3,
         out_specs=(anywhere,) * 3,
-        scratch_shapes=[pltpu.SemaphoreType.DMA((3,))],
+        scratch_shapes=[pltpu.VMEM(r.shape, r.dtype) for r in results]
+        + [pltpu.SemaphoreType.DMA((2, 3))],
     )(*results)
 
 

time: 163 us -> 138 us (0.85)
  Pallas kernels: 162 us -> 137 us
    pallas_call x1, Pallas kernels: 25 us -> 1.88 us  [hand_out(): pl.pallas_call(hand_out_kernel, out_shape=tuple((jax.ShapeDtypeStruct(r.s...]
    pallas_call x1, Pallas kernels: 137 us -> 135 us  [layer(): pl.pallas_call(functools.partial(layer_kernel, n), out_shape=(jax.ShapeDt...]
where the time goes in v3:
time: 138 us; the launch traced here: 137 us
  Pallas kernels  137 us (99%)
    pallas_call x1, Pallas kernels, layer(): pl.pallas_call(functools.partial(layer_kernel, n), out_shape=(jax.ShapeDt...  135 us

profile of v3, /device:TPU:0, one launch (start us, length us, event | category | flops | bytes accessed | tf_op | source)
XLA Modules:
  0.0 137.3 jit_solution(14188740285768124840)
XLA Ops:
  0.6 134.8 %shard_map.175 = (bf16[32,4096]{1,0:T(8,128)(2,1)}, bf16[16,16,512]{2,1,0:T(8,128)(2,1)}, bf16[16,16,512]{2,1,0:T(8,128)(2,1)}) custom-call(s32[1,32]{1,0:T(1,128)} %len_ref.1, s32[1,256]{1,0:T(1,128)} %order_ref.1, s32[1,16]{1,0:T(1,128)} %mig_page_ref.1, s32[1,16]{1,0:T(1,128)} %bitcast.11, s32[8,32]{1,0:T(8,128)} %bitcast.9, f32[8,32]{1,0:T(8,128)} %bitcast.10, ...), custom_call_target="tpu_custom_call" | custom-call | tf_op jit(solution)/shard_map/pallas_call | solution.py:462
  135.4 1.9 %shard_map.176 = (bf16[32,4096]{1,0:T(8,128)(2,1)}, bf16[16,16,512]{2,1,0:T(8,128)(2,1)}, bf16[16,16,512]{2,1,0:T(8,128)(2,1)}) custom-call(bf16[32,4096]{1,0:T(8,128)(2,1)} %get-tuple-element.6.a_ref, bf16[16,16,512]{2,1,0:T(8,128)(2,1)} %get-tuple-element.7.b_ref, bf16[16,16,512]{2,1,0:T(8,128)(2,1)} %get-tuple-element.8.c_ref), custom_call_target="tpu_custom_call" | custom-call | tf_op jit(solution)/shard_map/pallas_call | solution.py:528

commit v4 on v3

--- a/solution.py
+++ b/solution.py
@@ -253,6 +253,34 @@
             crecv[r, gi, b].astype(jnp.float32) + yrecv[r, gi].astype(jnp.float32)
         ).astype(jnp.bfloat16)
 
+    def line_copy(gi):
+        step = jnp.where(gi > g, 1, -1)
+        slot = jnp.where((step < 0) & (g + step == gi), G, gi)
+        return remote(yrecv.at[0, gi], zrecv.at[0, slot], rs.at[0, 4, gi], rs.at[0, 5, slot],
+                      dev(g + step, b, c))
+
+    def line_arrival(slot):
+        return remote(zrecv.at[0, slot], zrecv.at[0, slot], rs.at[0, 4, 0], rs.at[0, 5, slot],
+                      dev(g, b, 1 - c))
+
+    def starts_line(gi):
+        return ((gi > g) & (g == 0)) | ((gi < g) & (g == G - 1))
+
+    def line_stage(gi):
+        line_arrival(gi).wait_recv()
+        yrecv[0, gi] = (
+            yrecv[0, gi].astype(jnp.float32) + zrecv[0, gi].astype(jnp.float32)
+        ).astype(jnp.bfloat16)
+        line_copy(gi).start()
+
+    def collect_line():
+        acc[...] = yrecv[0, g].astype(jnp.float32)
+        for slot, there in ((g, g > 0), (G, g < G - 1)):
+            @pl.when(there)
+            def _():
+                line_arrival(slot).wait_recv()
+                acc[...] += zrecv[0, slot].astype(jnp.float32)
+
     def collect(r):
         acc[...] = yrecv[r, g].astype(jnp.float32)
 
@@ -289,16 +317,24 @@
         def _():
             core_stage(0, near(G - t))
 
+        @pl.when(t >= 3)
+        def _():
+            gi = near(G + 2 - t)
+
+            @pl.when(jnp.logical_not(starts_line(gi)))
+            def _():
+                line_stage(gi)
+
         @pl.when(t >= 2)
         def _():
             gi = near(G + 1 - t)
             y_stage(0, gi)
 
-            @pl.when(t <= G)
+            @pl.when(starts_line(gi))
             def _():
-                z_copy(0, gi, g).start()
-
-    collect(0)
+                line_copy(gi).start()
+
+    collect_line()
     load_hidden.wait()
     load_gain.wait()
     middle = (hidden_ref[...].astype(jnp.float32) + acc[...]).astype(jnp.bfloat16)
@@ -442,8 +478,8 @@
     @pl.loop(1, G)
     def _(i):
         gi = lax.rem(g + i, G)
-        for r in range(2):
-            z_copy(r, gi, g).wait_send()
+        line_copy(gi).wait_send()
+        z_copy(1, gi, g).wait_send()
 
 
 def layer(n, lengths, page_order, mig_pages, mig_dest, ids, weights, queries, fresh_keys,
@@ -477,7 +513,7 @@
             pltpu.VMEM((G, 2, 2, S, D), bf16),
             pltpu.VMEM((2, G, 2, S, D), bf16),
             pltpu.VMEM((2, G, S, D), bf16),
-            pltpu.VMEM((2, G, S, D), bf16),
+            pltpu.VMEM((2, G + 1, S, D), bf16),
             pltpu.VMEM((G, 2, 2, S, D), bf16),
             pltpu.VMEM((PLANE * S, FFW), bf16),
             pltpu.VMEM((S, D), bf16),
@@ -498,7 +534,7 @@
             dma((12,)),
             dma((2, n)), dma((2, n)), dma((n,)), dma((n,)),
             dma((n,)), dma((n,)), dma((n,)), dma((n,)),
-            dma((2, 6, G)),
+            dma((2, 6, G + 1)),
             dma((G, 2)), dma((G,)), dma((G, 2)), dma((G, 2, 2)),
         ],
         compiler_params=pltpu.CompilerParams(

time: 138 us -> 132 us (0.957)
  Pallas kernels: 137 us -> 131 us
    pallas_call x1, Pallas kernels: 135 us -> 129 us  [layer(): pl.pallas_call(functools.partial(layer_kernel, n), out_shape=(jax.ShapeDt...]
where the time goes in v4:
time: 132 us
  Pallas kernels  131 us (99%)
    pallas_call x1, Pallas kernels, layer(): pl.pallas_call(functools.partial(layer_kernel, n), out_shape=(jax.ShapeDt...  129 us

profile of v4, /device:TPU:0, one launch (start us, length us, event | category | flops | bytes accessed | tf_op | source)
XLA Modules:
  0.0 131.9 jit_solution(12972748092316611923)
XLA Ops:
  0.6 129.3 %shard_map.175 = (bf16[32,4096]{1,0:T(8,128)(2,1)}, bf16[16,16,512]{2,1,0:T(8,128)(2,1)}, bf16[16,16,512]{2,1,0:T(8,128)(2,1)}) custom-call(s32[1,32]{1,0:T(1,128)} %len_ref.1, s32[1,256]{1,0:T(1,128)} %order_ref.1, s32[1,16]{1,0:T(1,128)} %mig_page_ref.1, s32[1,16]{1,0:T(1,128)} %bitcast.11, s32[8,32]{1,0:T(8,128)} %bitcast.9, f32[8,32]{1,0:T(8,128)} %bitcast.10, ...), custom_call_target="tpu_custom_call" | custom-call | tf_op jit(solution)/shard_map/pallas_call | solution.py:498
  130.0 1.9 %shard_map.176 = (bf16[32,4096]{1,0:T(8,128)(2,1)}, bf16[16,16,512]{2,1,0:T(8,128)(2,1)}, bf16[16,16,512]{2,1,0:T(8,128)(2,1)}) custom-call(bf16[32,4096]{1,0:T(8,128)(2,1)} %get-tuple-element.6.a_ref, bf16[16,16,512]{2,1,0:T(8,128)(2,1)} %get-tuple-element.7.b_ref, bf16[16,16,512]{2,1,0:T(8,128)(2,1)} %get-tuple-element.8.c_ref), custom_call_target="tpu_custom_call" | custom-call | tf_op jit(solution)/shard_map/pallas_call | solution.py:564

commit v5 on v4

--- a/solution.py
+++ b/solution.py
@@ -79,8 +79,9 @@
     for k in range(ids_ref.shape[0]):
         table = table + jnp.where(experts == ids_ref[k:k + 1, :], weights_ref[k:k + 1, :], 0.0)
     table = jnp.concatenate([table, jnp.zeros((128, 128 - S), jnp.float32)], axis=1)
-    gate_ref[...] = table.T[0:S, :]
-    gates[me] = gate_ref[...]
+    for e in range(n):
+        gate_ref[e] = jnp.broadcast_to(table[e:e + 1, :], (8, 128))
+    gates[me] = gate_ref[me]
 
     def near(t):
         closest = jnp.minimum(g, G - 1 - g)
@@ -101,7 +102,7 @@
                       arecv.at[part_no, slot], {"ep": peer})
 
     def gate_copy(slot, peer):
-        return remote(gate_ref, gates.at[slot], gsend.at[peer], grecv.at[slot], {"ep": peer})
+        return remote(gate_ref.at[peer], gates.at[slot], gsend.at[peer], grecv.at[slot], {"ep": peer})
 
     def key_copy(slot, peer):
         return remote(mk_ref.at[peer], ak_ref.at[slot], ksend.at[peer], krecv.at[slot],
@@ -423,9 +424,19 @@
                              preferred_element_type=jnp.float32)
                 act[:, pl.ds(at, half)] = (gate * jax.nn.sigmoid(gate) * up).astype(jnp.bfloat16)
 
-            table = gates[pl.ds(gi * PLANE, PLANE)].reshape(block_rows, gates.shape[2])
-            column = lax.broadcasted_iota(jnp.int32, table.shape, 1)
-            chosen = jnp.sum(jnp.where(column == me, table, 0.0), axis=1, keepdims=True)
+            tiles = gates[pl.ds(gi * PLANE, PLANE)]
+            token = lax.broadcasted_iota(jnp.int32, (S, 128), 0)
+            same = token == lax.broadcasted_iota(jnp.int32, (S, 128), 1)
+            chosen = jnp.concatenate(
+                [
+                    jnp.sum(
+                        jnp.where(same, jnp.broadcast_to(tiles[j, 0:1, :], (S, 128)), 0.0),
+                        axis=1, keepdims=True,
+                    )
+                    for j in range(PLANE)
+                ],
+                axis=0,
+            )
             for j in range(D // tile):
                 y = jnp.dot(act[...], wd[:, j * tile:(j + 1) * tile],
                             preferred_element_type=jnp.float32)
@@ -509,7 +520,7 @@
             pltpu.VMEM(wgu.shape, bf16),
             pltpu.VMEM(wd.shape, bf16),
             pltpu.VMEM((n, S, wo.shape[0]), bf16),
-            pltpu.VMEM((n, S, 128), jnp.float32),
+            pltpu.VMEM((n, 8, 128), jnp.float32),
             pltpu.VMEM((G, 2, 2, S, D), bf16),
             pltpu.VMEM((2, G, 2, S, D), bf16),
             pltpu.VMEM((2, G, S, D), bf16),
@@ -528,7 +539,7 @@
             pltpu.VMEM((S, width), jnp.float32),
             pltpu.VMEM(pages, bf16),
             pltpu.VMEM(pages, bf16),
-            pltpu.VMEM((S, 128), jnp.float32),
+            pltpu.VMEM((n, 8, 128), jnp.float32),
             pltpu.VMEM(hidden.shape, bf16),
             pltpu.VMEM(gain.shape, jnp.float32),
             dma((12,)),

time: 132 us -> 128 us (0.970)
  Pallas kernels: 131 us -> 127 us
    pallas_call x1, Pallas kernels: 129 us -> 125 us  [layer(): pl.pallas_call(functools.partial(layer_kernel, n), out_shape=(jax.ShapeDt...]
where the time goes in v5:
time: 128 us
  Pallas kernels  127 us (99%)
    pallas_call x1, Pallas kernels, layer(): pl.pallas_call(functools.partial(layer_kernel, n), out_shape=(jax.ShapeDt...  125 us

profile of v5, /device:TPU:0, one launch (start us, length us, event | category | flops | bytes accessed | tf_op | source)
XLA Modules:
  0.0 127.6 jit_solution(5926056532492514250)
XLA Ops:
  0.6 125.1 %shard_map.175 = (bf16[32,4096]{1,0:T(8,128)(2,1)}, bf16[16,16,512]{2,1,0:T(8,128)(2,1)}, bf16[16,16,512]{2,1,0:T(8,128)(2,1)}) custom-call(s32[1,32]{1,0:T(1,128)} %len_ref.1, s32[1,256]{1,0:T(1,128)} %order_ref.1, s32[1,16]{1,0:T(1,128)} %mig_page_ref.1, s32[1,16]{1,0:T(1,128)} %bitcast.11, s32[8,32]{1,0:T(8,128)} %bitcast.9, f32[8,32]{1,0:T(8,128)} %bitcast.10, ...), custom_call_target="tpu_custom_call" | custom-call | tf_op jit(solution)/shard_map/pallas_call | solution.py:509
  125.7 1.9 %shard_map.176 = (bf16[32,4096]{1,0:T(8,128)(2,1)}, bf16[16,16,512]{2,1,0:T(8,128)(2,1)}, bf16[16,16,512]{2,1,0:T(8,128)(2,1)}) custom-call(bf16[32,4096]{1,0:T(8,128)(2,1)} %get-tuple-element.6.a_ref, bf16[16,16,512]{2,1,0:T(8,128)(2,1)} %get-tuple-element.7.b_ref, bf16[16,16,512]{2,1,0:T(8,128)(2,1)} %get-tuple-element.8.c_ref), custom_call_target="tpu_custom_call" | custom-call | tf_op jit(solution)/shard_map/pallas_call | solution.py:575
